TPU v7x, 128 devices: a whole 4x4x4 slice. The times are simulated.
128 devices in a mesh: seq: 16 (over z_hi, y, core), tp: 8 (over x, z_lo).
Axes of the slice: x: 4, y: 4, z: 4 (z_hi: 2, z_lo: 2; z = z_hi * 2 + z_lo), core: 2. Of those that a mesh axis runs over, the one named last changes fastest.
Arguments:
- temporal_out: bfloat16 [16384, 4096], P('seq', 'tp'), may hold values from -6 to 6
- context_weight: bfloat16 [4096, 1024], P('tp'), may hold values from -0.125 to 0.125
- text_ids: int32 [16384], P('seq'), may hold values from 0 to 16383
- code_ids: int32 [16384, 7], P('seq'), may hold values from 0 to 2047
- text_table: bfloat16 [16384, 1024], P(None, 'tp'), may hold values from -40 to 40
- code_tables: bfloat16 [7, 2048, 1024], P(None, None, 'tp'), may hold values from -40 to 40
- norm_gain: float32 [1024], replicated, may hold values from 0.5 to 1.5
- gate_weight: bfloat16 [1024, 2048], replicated, may hold values from -0.1875 to 0.1875
- up_weight: bfloat16 [1024, 2048], replicated, may hold values from -0.1875 to 0.1875
- hidden_grad: bfloat16 [16384, 8, 2048], P(('seq', 'tp')), may hold values from -0.75 to 0.75
- stream_grad: bfloat16 [16384, 8, 1024], P(('seq', 'tp')), may hold values from -0.75 to 0.75
Outputs:
- gate_grad: float32 [1024, 2048], P(('seq', 'tp'))
- up_grad: float32 [1024, 2048], P(('seq', 'tp'))
- gain_grad: float32 [1024], P(('seq', 'tp'))
- text_grad: float32 [16384, 1024], P('seq', 'tp')
- code_grad: float32 [7, 2048, 1024], P(None, 'seq', 'tp')
- context_grad: bfloat16 [16384, 1024], P(('seq', 'tp'))
All inputs are finite; a program needn't handle non-finite values.
Results may differ from a plain program's by a relative error of at most 0.04.
Values may be sent and summed in bfloat16 or wider, within the bound.
A program may use at most 128 MiB of HBM per device.

v0:
```python
import jax
import jax.numpy as jnp
from jax import lax
from jax.sharding import PartitionSpec as P

EPSILON = 1e-05


def on_device(
    temporal_out,
    context_weight,
    text_ids,
    code_ids,
    text_table,
    code_tables,
    norm_gain,
    gate_weight,
    up_weight,
    hidden_grad,
    stream_grad,
):
    code_count = code_tables.shape[0]
    card_size = code_tables.shape[1]
    own_frames = hidden_grad.shape[0]
    step_count = hidden_grad.shape[1]
    model_width = gate_weight.shape[0]
    hidden_width = gate_weight.shape[1]
    code_offsets = jnp.arange(code_count, dtype=jnp.int32)[None, :] * card_size
    text_rows = jnp.take(text_table, text_ids, axis=0)
    code_rows = jnp.take(
        code_tables.reshape(code_count * card_size, -1), code_ids + code_offsets, axis=0
    )
    embedded = jnp.concatenate([text_rows[:, None, :], code_rows], axis=1)
    partial_value = jnp.dot(temporal_out, context_weight, preferred_element_type=jnp.float32)
    context_slice = lax.psum_scatter(
        partial_value.astype(jnp.bfloat16), "tp", scatter_dimension=1, tiled=True
    ).astype(jnp.float32)
    feature_rows = (context_slice[:, None, :] + embedded.astype(jnp.float32)).astype(jnp.bfloat16)
    depth_in = lax.all_to_all(feature_rows, "tp", split_axis=0, concat_axis=2, tiled=True)
    depth_rows = depth_in.reshape(-1, model_width).astype(jnp.float32)
    inv_rms = lax.rsqrt(jnp.mean(depth_rows * depth_rows, axis=1, keepdims=True) + EPSILON)
    unit_rows = depth_rows * inv_rms
    normed = (unit_rows * norm_gain).astype(jnp.bfloat16)
    gate_values = jnp.dot(normed, gate_weight, preferred_element_type=jnp.float32)
    up_values = jnp.dot(normed, up_weight, preferred_element_type=jnp.float32)
    gate_sigmoid = jax.nn.sigmoid(gate_values)
    upstream = hidden_grad.reshape(-1, hidden_width).astype(jnp.float32)
    gate_back = (
        upstream * up_values * gate_sigmoid * (1.0 + gate_values * (1.0 - gate_sigmoid))
    ).astype(jnp.bfloat16)
    up_back = (upstream * gate_values * gate_sigmoid).astype(jnp.bfloat16)
    transposed = (((1,), (1,)), ((), ()))
    normed_back = lax.dot_general(
        gate_back, gate_weight, transposed, preferred_element_type=jnp.float32
    )
    normed_back = normed_back + lax.dot_general(
        up_back, up_weight, transposed, preferred_element_type=jnp.float32
    )
    gain_part = jnp.sum(normed_back * unit_rows, axis=0)
    scaled_back = normed_back * norm_gain
    stream_rows = stream_grad.reshape(-1, model_width).astype(jnp.float32)
    depth_back = stream_rows + inv_rms * (
        scaled_back - unit_rows * jnp.mean(scaled_back * unit_rows, axis=1, keepdims=True)
    )
    depth_grid = depth_back.astype(jnp.bfloat16).reshape(own_frames, step_count, model_width)
    context_grad = jnp.sum(depth_grid.astype(jnp.float32), axis=1).astype(jnp.bfloat16)
    over_rows = (((0,), (0,)), ((), ()))
    gate_term = lax.dot_general(normed, gate_back, over_rows, preferred_element_type=jnp.float32)
    up_term = lax.dot_general(normed, up_back, over_rows, preferred_element_type=jnp.float32)
    gate_grad, up_grad, gain_grad = (
        lax.psum_scatter(gate_term, ("seq", "tp"), scatter_dimension=0, tiled=True),
        lax.psum_scatter(up_term, ("seq", "tp"), scatter_dimension=0, tiled=True),
        lax.psum_scatter(gain_part, ("seq", "tp"), scatter_dimension=0, tiled=True),
    )
    feature_grid = lax.all_to_all(depth_grid, "tp", split_axis=2, concat_axis=0, tiled=True)
    feature_float = feature_grid.astype(jnp.float32)
    feature_width = feature_float.shape[2]
    text_part = jax.ops.segment_sum(feature_float[:, 0], text_ids, num_segments=text_table.shape[0])
    code_part = jax.ops.segment_sum(
        feature_float[:, 1:].reshape(-1, feature_width),
        (code_ids + code_offsets).reshape(-1),
        num_segments=code_count * card_size,
    )
    text_grad, code_grad = (
        lax.psum_scatter(
            text_part.astype(jnp.bfloat16), "seq", scatter_dimension=0, tiled=True
        ).astype(jnp.float32),
        lax.psum_scatter(
            code_part.reshape(code_count, card_size, feature_width).astype(jnp.bfloat16),
            "seq",
            scatter_dimension=1,
            tiled=True,
        ).astype(jnp.float32),
    )
    return (gate_grad, up_grad, gain_grad, text_grad, code_grad, context_grad)


def solution(mesh):
    return jax.shard_map(
        on_device,
        mesh=mesh,
        in_specs=(
            P("seq", "tp"),
            P("tp", None),
            P("seq"),
            P("seq", None),
            P(None, "tp"),
            P(None, None, "tp"),
            P(),
            P(),
            P(),
            P(("seq", "tp"), None, None),
            P(("seq", "tp"), None, None),
        ),
        out_specs=(
            P(("seq", "tp"), None),
            P(("seq", "tp"), None),
            P(("seq", "tp")),
            P("seq", "tp"),
            P(None, "seq", "tp"),
            P(("seq", "tp"), None),
        ),
        check_vma=False,
    )
```

profile of v0, /device:TPU:0, one launch (start us, length us, event | category | flops | bytes accessed | tf_op | source)
XLA Modules:
  0.0 1710.9 jit_solution(1976938276737392584)
XLA Ops:
  13.9 5.6 gather_fusion
  20.8 21.7 %gather_fusion.1 = bf16[7168,128]{1,0:T(8,128)(2,1)S(1)} fusion(bf16[14336,128]{1,0:T(8,128)(2,1)} %bitcast.57, s32[7168]{0:T(1024)S(1)} %broadcast_clamp_fusion), kind=kCustom, calls=%fused_computation.1 | custom fusion | bytes 3698688 | tf_op jit(solution)/shard_map/jit(_take)/gather | solution.py:30
  44.1 5.1 broadcast_select_fusion
  49.3 18.1 %reduce-scatter.16.cloned.1.call-done = bf16[128,1024]{1,0:T(8,128)(2,1)} async-done(((bf16[1024,1024]{1,0:T(8,128)(2,1)}), bf16[128,1024]{1,0:T(8,128)(2,1)}) %reduce-scatter.16.cloned.1.call-update) | async-done | bytes 262160
  69.7 31.1 %all_to_all.8 = bf16[1024,8,128]{2,1,0:T(8,128)(2,1)S(1)} all-to-all(bf16[1024,8,128]{2,1,0:T(8,128)(2,1)S(1)} %add_convert_fusion), channel_id=1, replica_groups=mesh['seq'=16,'tp'=8] {'tp'}, dimensions={0} | all-to-all | bytes 4194304 | tf_op jit(solution)/shard_map/all_to_all | solution.py:39
  105.9 8.2 fusion.4
  114.1 8.7 fusion.2
  122.8 6.1 fusion.16
  128.9 8.4 multiply_reduce_fusion
  143.8 3.6 all-to-all-start.1
  148.0 28.0 %all-to-all-done.1 = bf16[128,8,1024]{0,1,2:T(8,128)(2,1)S(1)} async-done(((bf16[128,8,1024]{0,1,2:T(8,128)(2,1)}), bf16[128,8,1024]{0,1,2:T(8,128)(2,1)S(1)}, u32[]{:S(2)}, u32[]{:S(2)}) %all-to-all-start.1) | async-done | bytes 2097184 | tf_op jit(solution)/shard_map/all_to_all | solution.py:75
  178.2 5.4 copy.63
  183.6 4.5 slice.13
  188.0 4.7 reshape.141
  192.7 42.3 %scatter_custom_fusion.1 = f32[14336,128]{1,0:T(8,128)} fusion(s32[7168]{0:T(1024)S(1)} %reshape.139, f32[7168,128]{1,0:T(8,128)} %reshape.141, f32[]{:T(128)} %constant.41.clone.1), kind=kCustom, calls=%fused_computation.23 | custom fusion | flops 917504 | bytes 7340544 | tf_op jit(solution)/shard_map/scatter-add | solution.py:79
  235.0 4.6 convert_element_type.105
  242.1 9.7 scatter_custom_fusion
  251.8 5.8 convert_element_type.103
  259.4 9.1 fusion.15
  268.6 9.0 fusion.14
  277.6 65.0 %all-reduce = f32[1024]{0:T(1024)S(1)} all-reduce(f32[1024]{0:T(1024)S(1)} %get-tuple-element.7), channel_id=5, replica_groups=mesh['seq'=16,'tp'=8] {'seq','tp'}, use_global_device_ids=true, to_apply=%region_6.7.clone | all-reduce | flops 1024 | bytes 8192
  344.9 55.4 %reduce-scatter.12.cloned.1.call-done = bf16[1024,128]{1,0:T(8,128)(2,1)} async-done(((bf16[16384,128]{1,0:T(8,128)(2,1)}), bf16[1024,128]{1,0:T(8,128)(2,1)}) %reduce-scatter.12.cloned.1.call-update) | async-done | bytes 262160 | tf_op jit(solution)/shard_map/reduce_scatter | solution.py:85
  402.1 652.5 %reduce-scatter.10.cloned.1.call-done = f32[8,2048]{1,0:T(8,128)} async-done(((f32[1024,2048]{1,0:T(8,128)}), f32[8,2048]{1,0:T(8,128)}) %reduce-scatter.10.cloned.1.call-update) | async-done | bytes 65552 | tf_op jit(solution)/shard_map/reduce_scatter | solution.py:72
  1054.6 649.8 %reduce-scatter.8.cloned.1.call-done = f32[8,2048]{1,0:T(8,128)} async-done(((f32[1024,2048]{1,0:T(8,128)}), f32[8,2048]{1,0:T(8,128)}) %reduce-scatter.8.cloned.1.call-update) | async-done | bytes 65552 | tf_op jit(solution)/shard_map/reduce_scatter | solution.py:71
  (70 shorter events, 34.5 us)
Async XLA Ops:
  7.2 1.2 copy-start
  7.2 60.1 %reduce-scatter.16.cloned.1.call-start = ((), (), s32[]{:S(2)}) async-start(), calls=%async_computation.11 | async-start | bytes 2359296
  10.9 2.6 copy-start.5
  10.9 3.0 copy-start.7
  100.8 1.8 copy-start.6
  102.3 2.2 copy-start.9
  102.6 3.2 copy-start.8
  105.9 8.2 copy-start.3
  105.9 8.2 copy-start.10
  122.8 6.1 copy-start.11
  128.9 8.5 copy-start.2
  143.8 32.2 %all-to-all-start.1 = ((bf16[128,8,1024]{0,1,2:T(8,128)(2,1)}), bf16[128,8,1024]{0,1,2:T(8,128)(2,1)S(1)}, u32[]{:S(2)}, u32[]{:S(2)}) async-start(bf16[128,8,1024]{0,1,2:T(8,128)(2,1)} %copy.62), calls=%async_computation.3 | async-start | bytes 4194304 | tf_op jit(solution)/shard_map/all_to_all | solution.py:75
  147.4 195.8 %reduce-scatter.14.cloned.1.call-start = ((), (), s32[]{:S(2)}) async-start(), calls=%async_computation.10 | async-start | bytes 3899392 | tf_op jit(solution)/shard_map/reduce_scatter | solution.py:88
  239.6 160.8 %reduce-scatter.12.cloned.1.call-start = ((), (), s32[]{:S(2)}) async-start(), calls=%async_computation.9 | async-start | bytes 4456448 | tf_op jit(solution)/shard_map/reduce_scatter | solution.py:85
  257.7 1.7 copy-start.4
  257.7 796.9 %reduce-scatter.10.cloned.1.call-start = ((), (), s32[]{:S(2)}) async-start(), calls=%async_computation.8 | async-start | bytes 8454144 | tf_op jit(solution)/shard_map/reduce_scatter | solution.py:72
  268.5 1435.8 %reduce-scatter.8.cloned.1.call-start = ((), (), s32[]{:S(2)}) async-start(), calls=%async_computation.7 | async-start | bytes 8454144 | tf_op jit(solution)/shard_map/reduce_scatter | solution.py:71
  277.6 1426.8 %copy-start.1 = (bf16[1024,512]{1,0:T(8,128)(2,1)S(1)}, bf16[1024,512]{1,0:T(8,128)(2,1)}, u32[]{:S(2)}) copy-start(bf16[1024,512]{1,0:T(8,128)(2,1)} %param.11) | copy-start | bytes 3145732
Sparse Core Ops, SparseCore 0:
  13.6 53.6 reduce-scatter.15
  239.7 77.3 reduce-scatter.13
  321.1 79.1 reduce-scatter.11
  403.3 651.2 reduce-scatter.9
  1057.4 646.9 reduce-scatter.7
where the time goes:
time: 1710 us
  waiting for transfers between devices  1400 us (82%)
  blocking collectives  96.1 us (6%)
  other arithmetic  79.9 us (5%)
  local copies, waits for them, and re-layouts  61.3 us (4%)
  matrix products  52 us (3%)
    reduce_scatter x1, waiting for transfers between devices, on_device(): lax.psum_scatter(up_term, ('seq', 'tp'), scatter_dimension=0, tiled=True)  652 us
    reduce_scatter x1, waiting for transfers between devices, on_device(): lax.psum_scatter(gate_term, ('seq', 'tp'), scatter_dimension=0, tiled=True)  650 us
    unnamed x1, blocking collectives  65 us
    reduce_scatter x1, waiting for transfers between devices, on_device(): lax.psum_scatter(text_part.astype(jnp.bfloat16), 'seq', scatter_dimension...  55.4 us
    scatter-add x1, other arithmetic, on_device(): jax.ops.segment_sum(feature_float[:, 1:].reshape(-1, feature_width), (cod...  42.3 us
  transfers between devices with their start and end apart: 6, of which 5 were waited for; matrix products, arithmetic and copies ran while one was open for 4% of the time, Pallas kernels for 0%

commit v1 on v0

--- a/solution.py
+++ b/solution.py
@@ -1,9 +1,463 @@
+import functools
+
 import jax
 import jax.numpy as jnp
 from jax import lax
+from jax.experimental import pallas as pl
+from jax.experimental.pallas import tpu as pltpu
 from jax.sharding import PartitionSpec as P
 
 EPSILON = 1e-05
+
+MESH = pl.DeviceIdType.MESH
+F32 = jnp.float32
+BF16 = jnp.bfloat16
+VMEM_LIMIT = 60 * 1024 * 1024
+
+
+def position():
+    seq = lax.axis_index("seq")
+    tp = lax.axis_index("tp")
+    core = lax.rem(seq, 2)
+    y = lax.rem(lax.div(seq, 2), 4)
+    z_hi = lax.div(seq, 8)
+    x = lax.div(tp, 2)
+    z_lo = lax.rem(tp, 2)
+    return core, x, y, z_hi * 2 + z_lo
+
+
+def device_at(core, x, y, z):
+    seq = (lax.div(z, 2) * 4 + y) * 2 + core
+    tp = x * 2 + lax.rem(z, 2)
+    return (seq, tp)
+
+
+def step_to(value, by):
+    return lax.rem(value + by, 4)
+
+
+def greet(devices):
+    barrier = pltpu.get_barrier_semaphore()
+    for device in devices:
+        pl.semaphore_signal(barrier, inc=1, device_id=device, device_id_type=MESH)
+    pl.semaphore_wait(barrier, len(devices))
+
+
+def add_blocks(count, target, sources):
+    def body(i, carry):
+        total = sources[0](i)[...].astype(F32)
+        for source in sources[1:]:
+            total = total + source(i)[...].astype(F32)
+        ref = target(i)
+        ref[...] = total.astype(ref.dtype)
+        return carry
+
+    lax.fori_loop(0, count, body, 0)
+
+
+class Copies:
+    def __init__(self, send_sems, recv_sems):
+        self.send_sems, self.recv_sems, self.made = send_sems, recv_sems, []
+
+    def send(self, source, target, device):
+        at = len(self.made)
+        copy = pltpu.make_async_remote_copy(
+            src_ref=source,
+            dst_ref=target,
+            send_sem=self.send_sems.at[at],
+            recv_sem=self.recv_sems.at[at],
+            device_id=device,
+            device_id_type=MESH,
+        )
+        copy.start()
+        self.made.append(copy)
+        return copy
+
+    def finish(self):
+        for copy in self.made:
+            copy.wait_send()
+
+
+class Ring:
+    def __init__(self, copies, here, device, part, pass_on, direct, ended):
+        self.copies, self.here, self.device, self.part = copies, here, device, part
+        self.pass_on, self.direct, self.ended = pass_on, direct, ended
+
+    def first(self):
+        up, down, far = (step_to(self.here, by) for by in (1, 3, 2))
+        up_device, down_device = self.device(up), self.device(down)
+        send = self.copies.send
+        self.from_down = send(self.part(far, 0), self.pass_on(0), up_device)
+        self.from_up = send(self.part(far, 1), self.pass_on(1), down_device)
+        self.near = [
+            send(self.part(up, 1), self.direct(1), up_device),
+            send(self.part(down, 0), self.direct(0), down_device),
+        ]
+
+    def second(self, add):
+        up, down = step_to(self.here, 1), step_to(self.here, 3)
+        self.from_down.wait_recv()
+        add(self.part(up, 0), [self.part(up, 0), self.pass_on(0)])
+        last_up = self.copies.send(self.part(up, 0), self.ended(0), self.device(up))
+        self.from_up.wait_recv()
+        add(self.part(down, 1), [self.part(down, 1), self.pass_on(1)])
+        last_down = self.copies.send(self.part(down, 1), self.ended(1), self.device(down))
+        self.last = [last_up, last_down]
+
+    def third(self, add, out):
+        for copy in self.near + self.last:
+            copy.wait_recv()
+        for half in (0, 1):
+            add(out(half), [self.part(self.here, half), self.direct(half), self.ended(half)])
+
+
+def reduce_kernel(
+    normed, gate_back, up_back, gain, tables,
+    gate_out, up_out, gain_out, text_out, code_out,
+    turned, term, pair, x_pass, x_direct, x_ended, z_term, z_pass, z_direct, z_ended,
+    y_term, y_pass, y_direct, y_ended, own, other, t_pass, t_direct, t_ended, t_sum, t_last,
+    gain_own, gain_in, local_sem, send_sems, recv_sems,
+):
+    core, x, y, z = position()
+    half_width = term.shape[-1] // 2
+    text_rows = text_out.shape[0]
+    table_rows = own.shape[2]
+    half_rows = table_rows // 2
+    z_hi = lax.div(z, 2)
+    sibling = device_at(1 - core, x, y, z)
+    x_device = lambda at: device_at(core, at, y, z)
+    y_device = lambda at: device_at(core, x, at, z)
+    z_device = lambda at: device_at(core, x, y, at)
+    greet(
+        [sibling]
+        + [x_device(step_to(x, by)) for by in (1, 2, 3)]
+        + [y_device(step_to(y, by)) for by in (1, 2, 3)]
+        + [z_device(step_to(z, by)) for by in (1, 2, 3)]
+    )
+    copies = Copies(send_sems, recv_sems)
+    halves = lambda half: pl.ds(half * half_width, half_width)
+
+    keep = pltpu.make_async_copy(tables.at[core], own, local_sem)
+    keep.start()
+    table_pairs = [
+        copies.send(tables.at[1 - core, i], other.at[i], sibling) for i in range(4)
+    ]
+    gain_own[0] = gain[...]
+    gain_copy = copies.send(gain_own.at[0], gain_in.at[0], sibling)
+
+    def make_term(q):
+        turned[...] = normed[:, q * 256 : (q + 1) * 256].T
+
+        def body(i, carry):
+            columns = pl.ds(pl.multiple_of(i * 256, 256), 256)
+            left = turned[...]
+            gate = jnp.dot(left, gate_back[:, columns], preferred_element_type=F32)
+            up = jnp.dot(left, up_back[:, columns], preferred_element_type=F32)
+            both = jnp.concatenate([gate.reshape(32, 8, 256), up.reshape(32, 8, 256)], axis=1)
+            both = both.astype(BF16).reshape(2, 2, 4, 2, 16, 256)
+            for low in range(2):
+                term[:, :, q * 2 + low, :, :, columns] = both[low]
+            return carry
+
+        lax.fori_loop(0, gate_back.shape[1] // 256, body, 0)
+
+    pair_copies = []
+
+    def send_pair(q):
+        rows = pl.ds(q * 2, 2)
+        pair_copies.append(copies.send(term.at[1 - core, :, rows], pair.at[:, rows], sibling))
+
+    def add_pair(q):
+        pair_copies[q].wait_recv()
+
+        def body(i, carry):
+            column, rest = lax.div(i, 4), lax.rem(i, 4)
+            row, low = q * 2 + lax.div(rest, 2), lax.rem(rest, 2)
+            here = term[core, column, row, low].astype(F32)
+            term[core, column, row, low] = (here + pair[column, row, low].astype(F32)).astype(BF16)
+            return carry
+
+        lax.fori_loop(0, 16, body, 0)
+
+    def add_four(out, refs):
+        def body(i, carry):
+            row, low = lax.div(i, 2), lax.rem(i, 2)
+            total = refs[0][row, low].astype(F32)
+            for ref in refs[1:]:
+                total = total + ref[row, low].astype(F32)
+            out[row, low] = total.astype(BF16)
+            return carry
+
+        lax.fori_loop(0, 4, body, 0)
+
+    def x_ring(q):
+        rows = pl.ds(q * 2, 2)
+        pick = lambda ref: lambda half: ref.at[rows, :, :, halves(half)]
+        return Ring(
+            copies, x, x_device,
+            lambda at, half: term.at[core, at, rows, :, :, halves(half)],
+            pick(x_pass), pick(x_direct), pick(x_ended),
+        )
+
+    x_rings = [x_ring(q) for q in range(4)]
+
+    def x_out(q):
+        def finish(out, refs):
+            def body(i, carry):
+                row, low = lax.div(i, 2), lax.rem(i, 2)
+                total = refs[0][row, low].astype(F32)
+                for ref in refs[1:]:
+                    total = total + ref[row, low].astype(F32)
+                z_term[q // 2 * 2 + low, q % 2 * 2 + row, :, out] = total.astype(BF16)
+                return carry
+
+            lax.fori_loop(0, 4, body, 0)
+
+        x_rings[q].third(finish, halves)
+
+    t_half = lambda half: pl.ds(half * half_rows, half_rows)
+    t_pick = lambda ref: lambda half: ref.at[:, t_half(half)]
+    t_ring = Ring(
+        copies, y, y_device,
+        lambda at, half: own.at[at, :, t_half(half)],
+        t_pick(t_pass), t_pick(t_direct), t_pick(t_ended),
+    )
+
+    def add_tables(out, refs):
+        def body(i, carry):
+            rows = pl.ds(pl.multiple_of(i * 64, 64), 64)
+            for hi in range(2):
+                total = refs[0][hi, rows].astype(F32)
+                for ref in refs[1:]:
+                    total = total + ref[hi, rows].astype(F32)
+                out[hi, rows] = total.astype(BF16)
+            return carry
+
+        lax.fori_loop(0, half_rows // 64, body, 0)
+
+    def pair_tables():
+        keep.wait()
+        for copy in table_pairs:
+            copy.wait_recv()
+
+        def body(i, carry):
+            rows = pl.ds(pl.multiple_of(lax.rem(i, table_rows // 64) * 64, 64), 64)
+            at = lax.div(i, table_rows // 64)
+            for hi in range(2):
+                total = own[at, hi, rows].astype(F32) + other[at, hi, rows].astype(F32)
+                own[at, hi, rows] = total.astype(BF16)
+            return carry
+
+        lax.fori_loop(0, 4 * table_rows // 64, body, 0)
+
+    def gain_round(index, device, here):
+        gain_own[index] = gain_own[index - 1] + gain_sum
+        return [
+            copies.send(gain_own.at[index], gain_in.at[index * 3 + by - 3], device(step_to(here, by)))
+            for by in (1, 2, 3)
+        ]
+
+    def gain_total(waited, slots):
+        for copy in waited:
+            copy.wait_recv()
+        total = gain_in[slots[0]]
+        for slot in slots[1:]:
+            total = total + gain_in[slot]
+        return total
+
+    make_term(0)
+    send_pair(0)
+    pair_tables()
+    t_ring.first()
+    make_term(1)
+    send_pair(1)
+    add_pair(0)
+    x_rings[0].first()
+    gain_sum = gain_total([gain_copy], [0])
+    gain_copies = gain_round(1, x_device, x)
+    make_term(2)
+    send_pair(2)
+    add_pair(1)
+    x_rings[1].first()
+    t_ring.second(add_tables)
+    make_term(3)
+    send_pair(3)
+    add_pair(2)
+    x_rings[2].first()
+    x_rings[0].second(add_four)
+    add_pair(3)
+    x_rings[3].first()
+    x_rings[1].second(add_four)
+    gain_sum = gain_total(gain_copies, [1, 2, 3])
+    gain_copies = gain_round(2, y_device, y)
+    x_out(0)
+    x_rings[2].second(add_four)
+    x_out(1)
+    t_ring.third(add_tables, lambda half: t_sum.at[:, t_half(half)])
+    t_copy = copies.send(t_sum.at[1 - z_hi], t_last, z_device(step_to(z, 2)))
+    x_rings[3].second(add_four)
+    x_out(2)
+    gain_sum = gain_total(gain_copies, [4, 5, 6])
+    gain_copies = gain_round(3, z_device, z)
+    x_out(3)
+
+    def add_few(out, refs):
+        for i in range(4):
+            total = refs[0][i].astype(F32)
+            for ref in refs[1:]:
+                total = total + ref[i].astype(F32)
+            out[i] = total.astype(BF16)
+
+    z_pick = lambda ref: lambda half: ref.at[:, :, halves(half)]
+    z_ring = Ring(
+        copies, z, z_device,
+        lambda at, half: z_term.at[at, :, :, halves(half)],
+        z_pick(z_pass), z_pick(z_direct), z_pick(z_ended),
+    )
+    z_ring.first()
+    z_ring.second(add_few)
+    z_ring.third(add_few, lambda half: y_term.at[:, :, halves(half)])
+
+    def add_one(out, refs):
+        total = refs[0][...].astype(F32)
+        for ref in refs[1:]:
+            total = total + ref[...].astype(F32)
+        out[...] = total.astype(BF16)
+
+    y_pick = lambda ref: lambda half: ref.at[:, halves(half)]
+    y_ring = Ring(
+        copies, y, y_device,
+        lambda at, half: y_term.at[at, :, halves(half)],
+        y_pick(y_pass), y_pick(y_direct), y_pick(y_ended),
+    )
+    y_ring.first()
+    t_copy.wait_recv()
+
+    def text_body(i, carry):
+        rows = pl.ds(pl.multiple_of(i * 64, 64), 64)
+        text_out[rows] = t_sum[z_hi, rows].astype(F32) + t_last[rows].astype(F32)
+        return carry
+
+    lax.fori_loop(0, text_rows // 64, text_body, 0)
+
+    def code_body(i, carry):
+        at = pl.ds(pl.multiple_of(i * 64, 64), 64)
+        rows = pl.ds(pl.multiple_of(text_rows + i * 64, 64), 64)
+        code_out[at] = t_sum[z_hi, rows].astype(F32) + t_last[rows].astype(F32)
+        return carry
+
+    lax.fori_loop(0, code_out.shape[0] // 64, code_body, 0)
+    gain_out[...] = gain_own[3] + gain_total(gain_copies, [7, 8, 9])
+    y_ring.second(add_one)
+
+    def finish_weights(out, refs):
+        total = refs[0][...].astype(F32)
+        for ref in refs[1:]:
+            total = total + ref[...].astype(F32)
+        gate_out[:, out] = total[:8]
+        up_out[:, out] = total[8:]
+
+    y_ring.third(finish_weights, halves)
+    copies.finish()
+
+
+def reduce_all(normed, gate_back, up_back, gain_part, tables):
+    features, width = normed.shape[1], gate_back.shape[1]
+    table_rows = tables.shape[3]
+    text_rows = table_rows * 8 // 15
+    out_rows = features // 128
+    bf = lambda *shape: pltpu.VMEM(shape, BF16)
+    vmem = pl.BlockSpec(memory_space=pltpu.VMEM)
+    return pl.pallas_call(
+        reduce_kernel,
+        out_shape=(
+            jax.ShapeDtypeStruct((out_rows, width), F32),
+            jax.ShapeDtypeStruct((out_rows, width), F32),
+            jax.ShapeDtypeStruct((8, 128), F32),
+            jax.ShapeDtypeStruct((text_rows, 128), F32),
+            jax.ShapeDtypeStruct((table_rows - text_rows, 128), F32),
+        ),
+        in_specs=[vmem] * 4 + [pl.BlockSpec(memory_space=pl.ANY)],
+        out_specs=(vmem,) * 5,
+        scratch_shapes=[
+            bf(256, normed.shape[0]),
+            bf(2, 4, 8, 2, 16, width),
+            bf(4, 8, 2, 16, width),
+            bf(8, 2, 16, width), bf(8, 2, 16, width), bf(8, 2, 16, width),
+            bf(4, 4, 16, width), bf(4, 16, width), bf(4, 16, width), bf(4, 16, width),
+            bf(4, 16, width), bf(16, width), bf(16, width), bf(16, width),
+            bf(4, 2, table_rows, 128), bf(4, 2, table_rows, 128),
+            bf(2, table_rows, 128), bf(2, table_rows, 128), bf(2, table_rows, 128),
+            bf(2, table_rows, 128), bf(table_rows, 128),
+            pltpu.VMEM((4, 8, 128), F32), pltpu.VMEM((10, 8, 128), F32),
+            pltpu.SemaphoreType.DMA,
+            pltpu.SemaphoreType.DMA((64,)),
+            pltpu.SemaphoreType.DMA((64,)),
+        ],
+        compiler_params=pltpu.CompilerParams(
+            collective_id=1, has_side_effects=True, vmem_limit_bytes=VMEM_LIMIT
+        ),
+        cost_estimate=pl.CostEstimate(flops=9_000_000_000, bytes_accessed=20_000_000, transcendentals=0),
+        name="reduce_all",
+    )(normed, gate_back, up_back, gain_part.reshape(8, 128), tables)
+
+
+def scatter_kernel(ids, grads, tables, rows, total, text_count, card, codes):
+    frames = grads.shape[0]
+    count = total.shape[0]
+
+    def clear(i, carry):
+        total[pl.ds(pl.multiple_of(i * 256, 256), 256)] = jnp.zeros((256, 128), F32)
+        return carry
+
+    lax.fori_loop(0, count // 256, clear, 0)
+
+    def widen(i, carry):
+        block = grads[pl.ds(i * 16, 16)].astype(F32).reshape(128, 128)
+        rows[pl.ds(pl.multiple_of(i * 128, 128), 128)] = block
+        return carry
+
+    lax.fori_loop(0, frames // 16, widen, 0)
+
+    def body(f, carry):
+        places = [ids[k * frames + f] for k in range(codes + 1)]
+        sums = [
+            total[pl.ds(places[k], 1)] + rows[pl.ds(f * (codes + 1) + k, 1)]
+            for k in range(codes + 1)
+        ]
+        for k in range(codes + 1):
+            total[pl.ds(places[k], 1)] = sums[k]
+        return carry
+
+    lax.fori_loop(0, frames, body, 0, unroll=4)
+
+    text_block, code_block = text_count // 16, card // 16
+    for block in range(16):
+        z_hi, y, core = block // 8, block // 2 % 4, block % 2
+        tables[core, y, z_hi, :text_block] = total[
+            block * text_block : (block + 1) * text_block
+        ].astype(BF16)
+        for c in range(codes):
+            first = text_count + c * card + block * code_block
+            tables[core, y, z_hi, pl.ds(text_block + c * code_block, code_block)] = total[
+                first : first + code_block
+            ].astype(BF16)
+
+
+def scatter_rows(ids, grads, text_count, card, codes):
+    rows = text_count // 16 + codes * card // 16
+    return pl.pallas_call(
+        functools.partial(scatter_kernel, text_count=text_count, card=card, codes=codes),
+        out_shape=jax.ShapeDtypeStruct((2, 4, 2, rows, 128), BF16),
+        in_specs=[pl.BlockSpec(memory_space=pltpu.SMEM), pl.BlockSpec(memory_space=pltpu.VMEM)],
+        out_specs=pl.BlockSpec(memory_space=pltpu.VMEM),
+        scratch_shapes=[
+            pltpu.VMEM((grads.shape[0] * (codes + 1), 128), F32),
+            pltpu.VMEM((text_count + codes * card, 128), F32),
+        ],
+        compiler_params=pltpu.CompilerParams(vmem_limit_bytes=VMEM_LIMIT),
+        name="scatter_rows",
+    )(ids, grads)
 
 
 def on_device(
@@ -64,34 +518,17 @@
     )
     depth_grid = depth_back.astype(jnp.bfloat16).reshape(own_frames, step_count, model_width)
     context_grad = jnp.sum(depth_grid.astype(jnp.float32), axis=1).astype(jnp.bfloat16)
-    over_rows = (((0,), (0,)), ((), ()))
-    gate_term = lax.dot_general(normed, gate_back, over_rows, preferred_element_type=jnp.float32)
-    up_term = lax.dot_general(normed, up_back, over_rows, preferred_element_type=jnp.float32)
-    gate_grad, up_grad, gain_grad = (
-        lax.psum_scatter(gate_term, ("seq", "tp"), scatter_dimension=0, tiled=True),
-        lax.psum_scatter(up_term, ("seq", "tp"), scatter_dimension=0, tiled=True),
-        lax.psum_scatter(gain_part, ("seq", "tp"), scatter_dimension=0, tiled=True),
-    )
     feature_grid = lax.all_to_all(depth_grid, "tp", split_axis=2, concat_axis=0, tiled=True)
-    feature_float = feature_grid.astype(jnp.float32)
-    feature_width = feature_float.shape[2]
-    text_part = jax.ops.segment_sum(feature_float[:, 0], text_ids, num_segments=text_table.shape[0])
-    code_part = jax.ops.segment_sum(
-        feature_float[:, 1:].reshape(-1, feature_width),
-        (code_ids + code_offsets).reshape(-1),
-        num_segments=code_count * card_size,
-    )
-    text_grad, code_grad = (
-        lax.psum_scatter(
-            text_part.astype(jnp.bfloat16), "seq", scatter_dimension=0, tiled=True
-        ).astype(jnp.float32),
-        lax.psum_scatter(
-            code_part.reshape(code_count, card_size, feature_width).astype(jnp.bfloat16),
-            "seq",
-            scatter_dimension=1,
-            tiled=True,
-        ).astype(jnp.float32),
-    )
+    places = jnp.concatenate(
+        [text_ids[None], code_ids.T + code_offsets.T + text_table.shape[0]], axis=0
+    ).reshape(-1)
+    tables = scatter_rows(places, feature_grid, text_table.shape[0], card_size, code_count)
+    gate_grad, up_grad, gain_sum, text_grad, code_sum = reduce_all(
+        normed, gate_back, up_back, gain_part, tables
+    )
+    own_place = lax.axis_index("seq") * lax.axis_size("tp") + lax.axis_index("tp")
+    gain_grad = lax.dynamic_slice_in_dim(gain_sum.reshape(-1), own_place * 8, 8)
+    code_grad = code_sum.reshape(code_count, -1, code_sum.shape[1])
     return (gate_grad, up_grad, gain_grad, text_grad, code_grad, context_grad)
 
 

time: 1710 us -> 304 us (0.18)
  waiting for transfers between devices: 1400 us -> 46.6 us
  Pallas kernels: 0 us -> 102 us
  other arithmetic: 79.9 us -> 12.6 us
  blocking collectives: 96.1 us -> 31.1 us
    reduce_scatter x4 -> x0, waiting for transfers between devices: 1360 us -> none  [the longest x1 652 us: on_device(): lax.psum_scatter(up_term, ('seq', 'tp'), scatter_dimension=0, tiled=True)]
    pallas_call x0 -> x2, Pallas kernels: none -> 102 us  [the longest x1 83.5 us: reduce_all(): pl.pallas_call(reduce_kernel, out_shape=(jax.ShapeDtypeStruct((out_rows,...]
    unnamed x1 -> x0, blocking collectives: 65 us -> none
    scatter-add x2 -> x0, other arithmetic: 52 us -> none  [the longest x1 42.3 us: on_device(): jax.ops.segment_sum(feature_float[:, 1:].reshape(-1, feature_width), (cod...]
    dot_general x2 -> x0, matrix products: 18.1 us -> none  [the longest x1 9.13 us: on_device(): lax.dot_general(normed, up_back, over_rows, preferred_element_type=jnp.fl...]
  transfers between devices with their start and end apart: 6 -> 2, of which waited for: 5 -> 2; matrix products, arithmetic and copies ran while one was open for 4% -> 12% of each run, Pallas kernels for 0% -> 0%
where the time goes in v1:
time: 304 us; the launch traced here: 302 us
  Pallas kernels  102 us (34%)
  local copies, waits for them, and re-layouts  53.4 us (18%)
  waiting for transfers between devices  46.6 us (15%)
  matrix products  37.8 us (12%)
  blocking collectives  31.1 us (10%)
  between operations  14.3 us (5%)
  other arithmetic  12.6 us (4%)
  starting transfers between devices  3.64 us (1%)
    pallas_call x1, Pallas kernels, reduce_all(): pl.pallas_call(reduce_kernel, out_shape=(jax.ShapeDtypeStruct((out_rows,...  83.5 us
    all_to_all x1, blocking collectives, on_device(): lax.all_to_all(feature_rows, 'tp', split_axis=0, concat_axis=2, tiled=True)  31.1 us
    all_to_all x1, waiting for transfers between devices, on_device(): lax.all_to_all(depth_grid, 'tp', split_axis=2, concat_axis=0, tiled=True)  28 us
    gather x2, local copies, waits for them, and re-layouts, on_device(): jnp.take(code_tables.reshape(code_count * card_size, -1), code_ids + code...  23.3 us
    pallas_call x1, Pallas kernels, scatter_rows(): pl.pallas_call(functools.partial(scatter_kernel, text_count=text_count, c...  18.9 us
    unnamed x2, waiting for transfers between devices  18.7 us
    unnamed x31, local copies, waits for them, and re-layouts  15 us
    dot_general x1, matrix products, on_device(): up_values = jnp.dot(normed, up_weight, preferred_element_type=jnp.float32)  11.6 us
  transfers between devices with their start and end apart: 2, of which 2 were waited for; matrix products, arithmetic and copies ran while one was open for 12% of the time, Pallas kernels for 0%

profile of v1, /device:TPU:0, one launch (start us, length us, event | category | flops | bytes accessed | tf_op | source)
XLA Modules:
  0.0 301.7 jit_solution(7182992871802419905)
XLA Ops:
  8.4 2.5 convolution_convert_fusion
  10.9 2.6 copy.59
  14.2 21.7 %gather_fusion.1 = bf16[7168,128]{1,0:T(8,128)(2,1)S(1)} fusion(bf16[14336,128]{1,0:T(8,128)(2,1)} %bitcast.61, s32[7168]{0:T(1024)S(1)} %broadcast_clamp_fusion), kind=kCustom, calls=%fused_computation.1 | custom fusion | bytes 3698688 | tf_op jit(solution)/shard_map/jit(_take)/gather | solution.py:484
  35.9 1.6 reshape.130
  37.8 5.8 %gather_fusion = bf16[1024,128]{1,0:T(8,128)(2,1)S(1)} fusion(bf16[16384,128]{1,0:T(8,128)(2,1)} %param.15, s32[1024]{0:T(1024)S(1)} %fusion.7), kind=kCustom, calls=%fused_computation | custom fusion | bytes 528384 | tf_op jit(solution)/shard_map/jit(_take)/gather | solution.py:483
  44.3 4.3 %broadcast_select_fusion = bf16[1024,7,128]{2,1,0:T(8,128)(2,1)} fusion(bf16[1024,7,128]{2,1,0:T(8,128)(2,1)S(1)} %copy-done.2, pred[1024,7]{1,0:T(8,128)(4,1)S(1)} %copy.51), kind=kLoop, calls=%fused_computation.19 | loop fusion | flops 917504 | bytes 3677184 | tf_op jit(solution)/shard_map/jit(_take)/select_n | solution.py:484
  48.7 18.6 %reduce-scatter.4.cloned.1.call-done = bf16[128,1024]{1,0:T(8,128)(2,1)} async-done(((bf16[1024,1024]{1,0:T(8,128)(2,1)}), bf16[128,1024]{1,0:T(8,128)(2,1)}) %reduce-scatter.4.cloned.1.call-update) | async-done | bytes 262160
  68.5 2.8 add_convert_fusion
  71.3 31.1 %all_to_all.27 = bf16[1024,8,128]{2,1,0:T(8,128)(2,1)S(1)} all-to-all(bf16[1024,8,128]{2,1,0:T(8,128)(2,1)S(1)} %add_convert_fusion), channel_id=1, replica_groups=mesh['seq'=16,'tp'=8] {'tp'}, dimensions={0} | all-to-all | bytes 4194304 | tf_op jit(solution)/shard_map/all_to_all | solution.py:493
  107.4 7.6 %fusion.4 = (bf16[1024,2048]{1,0:T(8,128)(2,1)S(1)}, f32[1024,2048]{1,0:T(8,128)}) fusion(bf16[128,8,2048]{2,1,0:T(8,128)(2,1)S(1)} %copy-done.8, bf16[1024,1024]{1,0:T(8,128)(2,1)S(1)} %multiply_convert_fusion.normed, bf16[1024,2048]{1,0:T(8,128)(2,1)S(1)} %copy-done.9), kind=kOutput, calls=%fused_computation.8 | convolution fusion | flops 4309647360 | bytes 23068672 | tf_op jit(solution)/shard_map/dot_general | solution.py:498
  115.0 11.6 %fusion.2.gate_back = bf16[1024,2048]{1,0:T(8,128)(2,1)} fusion(f32[1024,2048]{1,0:T(8,128)} %get-tuple-element.23, bf16[1024,1024]{1,0:T(8,128)(2,1)S(1)} %multiply_convert_fusion.normed, bf16[1024,2048]{1,0:T(8,128)(2,1)S(1)} %copy-done.10, bf16[128,8,2048]{2,1,0:T(8,128)(2,1)S(1)} %copy-done.8), kind=kOutput, calls=%fused_computation.6 | convolution fusion | flops 4318035968 | bytes 23068672 | tf_op jit(solution)/shard_map/dot_general | solution.py:499
  126.6 8.4 %fusion.10 = f32[1024,1024]{1,0:T(8,128)} fusion(bf16[1024,2048]{1,0:T(8,128)(2,1)} %fusion.2.gate_back, bf16[1024,2048]{1,0:T(8,128)(2,1)S(1)} %copy-done.9), kind=kOutput, calls=%fused_computation.37 | convolution fusion | flops 4294967296 | bytes 12582912 | tf_op jit(solution)/shard_map/dot_general | solution.py:507
  135.0 7.8 %multiply_reduce_fusion = (f32[1024]{0:T(1024)S(1)}, f32[1024]{0:T(1024)}, f32[1024,1024]{1,0:T(8,128)S(1)}) fusion(f32[128,8,8,128]{3,1,0,2:T(8,128)S(1)} %bitcast.62, f32[1024]{0:T(1024)S(1)} %copy-done.7, f32[1024]{0:T(1024)S(1)} %rsqrt.12, f32[1024,1024]{1,0:T(8,128)} %fusion.10, bf16[1024,2048]{1,0:T(8,128)(2,1)S(1)} %get-tuple-element.22.up_back, ...), kind=kOutput, calls=%fused_computation.13 | convolution fusion | flops 4302305280 | bytes 20987904 | tf_op jit(solution)/shard_map/dot_general | solution.py:510
  142.8 3.1 %fusion.8 = (bf16[128,1024]{1,0:T(8,128)(2,1)}, bf16[128,8,1024]{2,1,0:T(8,128)(2,1)S(1)}) fusion(f32[1024]{0:T(1024)S(1)} %broadcast_multiply_fusion, f32[128,8,8,128]{3,1,0,2:T(8,128)S(1)} %bitcast.63, f32[1024,1024]{1,0:T(8,128)S(1)} %get-tuple-element.24, f32[1024]{0:T(1024)S(1)} %copy-done.7, f32[1024]{0:T(1024)S(1)} %rsqrt.12, ...), kind=kLoop, calls=%fused_computation.36 | loop fusion | flops 9306112 | bytes 12857344 | tf_op jit(solution)/shard_map/reduce_sum | solution.py:520
  145.9 3.2 %copy.57 = bf16[128,8,1024]{0,1,2:T(8,128)(2,1)} copy(bf16[128,8,1024]{2,1,0:T(8,128)(2,1)S(1)} %get-tuple-element.19) | data formatting | bytes 4194304 | tf_op jit(solution)/shard_map/reshape | solution.py:519
  149.1 3.6 %all-to-all-start.1 = ((bf16[128,8,1024]{0,1,2:T(8,128)(2,1)}), bf16[128,8,1024]{0,1,2:T(8,128)(2,1)S(1)}, u32[]{:S(2)}, u32[]{:S(2)}) async-start(bf16[128,8,1024]{0,1,2:T(8,128)(2,1)} %copy.57), calls=%async_computation.1 | async-start | bytes 4194304 | tf_op jit(solution)/shard_map/all_to_all | solution.py:521
  153.4 28.0 %all-to-all-done.1 = bf16[128,8,1024]{0,1,2:T(8,128)(2,1)S(1)} async-done(((bf16[128,8,1024]{0,1,2:T(8,128)(2,1)}), bf16[128,8,1024]{0,1,2:T(8,128)(2,1)S(1)}, u32[]{:S(2)}, u32[]{:S(2)}) %all-to-all-start.1) | async-done | bytes 2097184 | tf_op jit(solution)/shard_map/all_to_all | solution.py:521
  181.4 3.2 %copy.58 = bf16[128,8,8,128]{3,1,0,2:T(8,128)(2,1)} copy(bf16[128,8,8,128]{0,1,3,2:T(8,128)(2,1)S(1)} %bitcast.65) | data formatting | bytes 4194304 | tf_op jit(solution)/shard_map/all_to_all | solution.py:521
  184.6 18.9 %scatter_rows.1.tables = bf16[2,4,2,1920,128]{4,3,2,1,0:T(8,128)(2,1)} custom-call(s32[8192]{0:T(1024)} %bitcast.69, bf16[1024,8,128]{2,1,0:T(8,128)(2,1)} %bitcast.64), custom_call_target="tpu_custom_call" | custom-call | tf_op jit(solution)/shard_map/scatter_rows/pallas_call | solution.py:449
  203.5 83.5 %reduce_all.1 = (f32[8,2048]{1,0:T(8,128)}, f32[8,2048]{1,0:T(8,128)}, f32[8,128]{1,0:T(8,128)}, f32[1024,128]{1,0:T(8,128)}, f32[896,128]{1,0:T(8,128)}) custom-call(bf16[1024,1024]{1,0:T(8,128)(2,1)} %copy-done.4, bf16[1024,2048]{1,0:T(8,128)(2,1)} %fusion.2.gate_back, bf16[1024,2048]{1,0:T(8,128)(2,1)} %copy-done.11, f32[8,128]{1,0:T(8,128)} %bitcast.72, ...), custom_call_target="tpu_custom_call" | custom-call | flops 8999999488 | bytes 20000000 | tf_op jit(solution)/shard_map/reduce_all/pallas_call | solution.py:371
  288.2 1.5 copy.80
  289.7 1.5 copy.81
  291.2 1.9 copy.82
  293.0 1.8 copy.83
  (51 shorter events, 11.0 us)
Async XLA Ops:
  7.2 1.2 copy-start
  7.2 60.1 %reduce-scatter.4.cloned.1.call-start = ((), (), s32[]{:S(2)}) async-start(), calls=%async_computation.3 | async-start | bytes 2359296
  10.9 2.6 copy-start.5
  14.2 23.6 %copy-start.6 = (s32[1024]{0:T(1024)S(1)}, s32[1024]{0:T(1024)}, u32[]{:S(2)}) copy-start(s32[1024]{0:T(1024)} %param.13) | copy-start | bytes 12292
  37.5 6.8 %copy-start.2 = (bf16[1024,7,128]{2,1,0:T(8,128)(2,1)S(1)}, bf16[1024,7,128]{2,1,0:T(8,128)(2,1)}, u32[]{:S(2)}) copy-start(bf16[1024,7,128]{2,1,0:T(8,128)(2,1)} %reshape.130) | copy-start | bytes 5505028
  102.3 1.8 copy-start.7
  103.9 2.2 copy-start.9
  104.2 3.2 %copy-start.8 = (bf16[128,8,2048]{2,1,0:T(8,128)(2,1)S(1)}, bf16[128,8,2048]{2,1,0:T(8,128)(2,1)}, u32[]{:S(2)}) copy-start(bf16[128,8,2048]{2,1,0:T(8,128)(2,1)} %param.20) | copy-start | bytes 12582916
  107.4 7.6 %copy-start.4 = (bf16[1024,1024]{1,0:T(8,128)(2,1)}, bf16[1024,1024]{1,0:T(8,128)(2,1)S(1)}, u32[]{:S(2)}) copy-start(bf16[1024,1024]{1,0:T(8,128)(2,1)S(1)} %multiply_convert_fusion.normed) | copy-start | bytes 6291460
  107.4 7.6 %copy-start.10 = (bf16[1024,2048]{1,0:T(8,128)(2,1)S(1)}, bf16[1024,2048]{1,0:T(8,128)(2,1)}, u32[]{:S(2)}) copy-start(bf16[1024,2048]{1,0:T(8,128)(2,1)} %param.19) | copy-start | bytes 12582916
  115.0 20.0 %copy-start.11 = (bf16[1024,2048]{1,0:T(8,128)(2,1)}, bf16[1024,2048]{1,0:T(8,128)(2,1)S(1)}, u32[]{:S(2)}) copy-start(bf16[1024,2048]{1,0:T(8,128)(2,1)S(1)} %get-tuple-element.22.up_back) | copy-start | bytes 12582916
  135.0 7.8 %copy-start.3 = (bf16[128,8,1024]{2,1,0:T(8,128)(2,1)S(1)}, bf16[128,8,1024]{2,1,0:T(8,128)(2,1)}, u32[]{:S(2)}) copy-start(bf16[128,8,1024]{2,1,0:T(8,128)(2,1)} %param.21) | copy-start | bytes 6291460
  149.1 32.3 %all-to-all-start.1 = ((bf16[128,8,1024]{0,1,2:T(8,128)(2,1)}), bf16[128,8,1024]{0,1,2:T(8,128)(2,1)S(1)}, u32[]{:S(2)}, u32[]{:S(2)}) async-start(bf16[128,8,1024]{0,1,2:T(8,128)(2,1)} %copy.57), calls=%async_computation.1 | async-start | bytes 4194304 | tf_op jit(solution)/shard_map/all_to_all | solution.py:521
  203.5 91.4 %copy-start.1 = (bf16[1024,512]{1,0:T(8,128)(2,1)S(1)}, bf16[1024,512]{1,0:T(8,128)(2,1)}, u32[]{:S(2)}) copy-start(bf16[1024,512]{1,0:T(8,128)(2,1)} %param.11) | copy-start | bytes 3145732
Sparse Core Ops, SparseCore 0:
  13.6 53.6 reduce-scatter.3

commit v2 on v1

--- a/solution.py
+++ b/solution.py
@@ -41,18 +41,6 @@
     for device in devices:
         pl.semaphore_signal(barrier, inc=1, device_id=device, device_id_type=MESH)
     pl.semaphore_wait(barrier, len(devices))
-
-
-def add_blocks(count, target, sources):
-    def body(i, carry):
-        total = sources[0](i)[...].astype(F32)
-        for source in sources[1:]:
-            total = total + source(i)[...].astype(F32)
-        ref = target(i)
-        ref[...] = total.astype(ref.dtype)
-        return carry
-
-    lax.fori_loop(0, count, body, 0)
 
 
 class Copies:
@@ -109,6 +97,339 @@
             copy.wait_recv()
         for half in (0, 1):
             add(out(half), [self.part(self.here, half), self.direct(half), self.ended(half)])
+
+
+class Exchange:
+    def __init__(self, copies, x, z_lo, device, chunk, landing, relay):
+        self.copies, self.x, self.z_lo, self.device = copies, x, z_lo, device
+        self.chunk, self.landing, self.relay = chunk, landing, relay
+        self.relays, self.arrivals = [], []
+
+    def place(self, by_x, by_z):
+        z_lo = self.z_lo if by_z == 0 else 1 - self.z_lo
+        return step_to(self.x, by_x) * 2 + z_lo
+
+    def start(self, by_x, by_z):
+        own, there = self.place(0, 0), self.place(by_x, by_z)
+        send = self.copies.send
+        if by_x == 2:
+            for half, by in ((0, 1), (1, 3)):
+                copy = send(self.chunk(there, half), self.relay(by_z, half), self.device(self.place(by, by_z)))
+                self.relays.append((copy, by_z, half))
+        else:
+            self.arrivals.append(send(self.chunk(there, None), self.landing(own, None), self.device(there)))
+
+    def forward(self):
+        for copy, by_z, half in self.relays:
+            copy.wait_recv()
+            came, by = ((3, 1), (1, 3))[half]
+            target = self.landing(self.place(came, by_z), half)
+            self.arrivals.append(
+                self.copies.send(self.relay(by_z, half), target, self.device(self.place(by, 0)))
+            )
+
+    def arrive(self):
+        for copy in self.arrivals:
+            copy.wait_recv()
+
+
+ORDER = ((2, 1), (2, 0), (1, 1), (3, 1), (1, 0), (3, 0), (0, 1), (0, 0))
+TILES = 4
+
+
+def front_kernel(
+    ids, text_table, code_tables, temporal, context_weight, gain, gate_weight, up_weight, hidden, stream,
+    normed_out, gate_out, up_out, gain_out, context_out, grid_out,
+    table, staged, table_sems, picked,
+    c_term, c_pass, c_direct, c_ended, c_pair, c_last, context,
+    e_send, e_in, e_relay, g_send, g_relay,
+    gate_w, up_w, hidden_in, stream_in, load_sems,
+    normed, gate_back, up_back, out_sems, unit, scale, back, context_grad, send_sems, recv_sems,
+):
+    core, x, y, z = position()
+    z_lo = lax.rem(z, 2)
+    own = x * 2 + z_lo
+    frames_all = temporal.shape[0]
+    frames = frames_all // 8
+    tile = frames // TILES
+    rows = tile * 8
+    half_rows = rows // 2
+    seq = lax.axis_index("seq")
+    device = lambda place: (seq, place)
+    copies = Copies(send_sems, recv_sems)
+
+    loads = []
+    for at, (source, target) in enumerate(
+        ((gate_weight, gate_w), (up_weight, up_w), (hidden, hidden_in), (stream, stream_in))
+    ):
+        loads.append(pltpu.make_async_copy(source, target, load_sems.at[at]))
+
+    block = staged.shape[1]
+    text_blocks = text_table.shape[0] // block
+    blocks = table.shape[0] // block
+
+    def load_block(i):
+        source = text_table if i < text_blocks else code_tables
+        first = (i if i < text_blocks else i - text_blocks) * block
+        return pltpu.make_async_copy(
+            source.at[pl.ds(first, block)], staged.at[i % 2], table_sems.at[i % 2]
+        )
+
+    block_loads = [load_block(i) for i in range(blocks)]
+    block_loads[0].start()
+    block_loads[1].start()
+    for load in loads:
+        load.start()
+    greet([device(lax.rem(own + by, 8)) for by in range(1, 8)])
+
+    def context_body(i, carry):
+        block_rows = pl.ds(pl.multiple_of(i * frames, frames), frames)
+        partial = jnp.dot(temporal[block_rows], context_weight[...], preferred_element_type=F32)
+        c_term[lax.div(i, 2), lax.rem(i, 2)] = partial.astype(BF16)
+        return carry
+
+    lax.fori_loop(0, 8, context_body, 0)
+    half_width = c_term.shape[-1] // 2
+    c_half = lambda half: pl.ds(half * half_width, half_width)
+    c_pick = lambda ref: lambda half: ref.at[:, :, c_half(half)]
+    c_ring = Ring(
+        copies, x, lambda at: device(at * 2 + z_lo),
+        lambda at, half: c_term.at[at, :, :, c_half(half)],
+        c_pick(c_pass), c_pick(c_direct), c_pick(c_ended),
+    )
+    c_ring.first()
+
+    def add_context(out, refs):
+        def body(i, carry):
+            at = pl.ds(pl.multiple_of(lax.rem(i, frames // 16) * 16, 16), 16)
+            low = lax.div(i, frames // 16)
+            total = refs[0][low, at].astype(F32)
+            for ref in refs[1:]:
+                total = total + ref[low, at].astype(F32)
+            out[low, at] = total.astype(BF16)
+            return carry
+
+        lax.fori_loop(0, frames // 8, body, 0)
+
+    for i in range(blocks):
+        block_loads[i].wait()
+
+        def widen(j, carry):
+            at = pl.multiple_of(j * 128, 128)
+            table[pl.ds(i * block + at, 128)] = staged[i % 2, pl.ds(at, 128)].astype(F32)
+            return carry
+
+        lax.fori_loop(0, block // 128, widen, 0)
+        if i + 2 < blocks:
+            block_loads[i + 2].start()
+
+    def gather(t, place, target):
+        def body(f, carry):
+            frame = place * frames + t * tile + f
+            for k in range(8):
+                picked[pl.ds(f * 8 + k, 1)] = table[pl.ds(ids[k * frames_all + frame], 1)]
+            return carry
+
+        lax.fori_loop(0, tile, body, 0, unroll=4)
+        target[...] = picked[...].astype(BF16)
+
+    def tile_rows(t, half):
+        if half is None:
+            return pl.ds(t * rows, rows)
+        return pl.ds(t * rows + half * half_rows, half_rows)
+
+    def exchange(t, send_ref, in_ref, relay_ref):
+        return Exchange(
+            copies, x, z_lo, device,
+            lambda place, half: send_ref.at[place, tile_rows(t, half)],
+            lambda place, half: in_ref.at[place, tile_rows(t, half)],
+            lambda by_z, half: relay_ref.at[t, by_z, half],
+        )
+
+    rows_in = [exchange(t, e_send, e_in, e_relay) for t in range(TILES)]
+    rows_back = [exchange(t, g_send, grid_out, g_relay) for t in range(TILES)]
+
+    def gather_tile(t):
+        for by_x, by_z in ORDER:
+            place = rows_in[t].place(by_x, by_z)
+            if (by_x, by_z) == (0, 0):
+                gather(t, place, e_in.at[place, tile_rows(t, None)])
+            else:
+                gather(t, place, e_send.at[place, tile_rows(t, None)])
+                rows_in[t].start(by_x, by_z)
+
+    gather_tile(0)
+    c_ring.second(add_context)
+    gather_tile(1)
+    rows_in[0].forward()
+    c_ring.third(add_context, lambda half: c_pair.at[:, :, c_half(half)])
+    c_copy = copies.send(c_pair.at[1 - z_lo], c_last, device(x * 2 + 1 - z_lo))
+    gather_tile(2)
+    rows_in[1].forward()
+    gather_tile(3)
+    rows_in[2].forward()
+    c_copy.wait_recv()
+
+    def context_total(i, carry):
+        at = pl.ds(pl.multiple_of(i * 16, 16), 16)
+        context[at] = c_pair[z_lo, at].astype(F32) + c_last[at].astype(F32)
+        return carry
+
+    lax.fori_loop(0, frames // 16, context_total, 0)
+
+    width = context.shape[1]
+    column_blocks = width // 128
+    gain_out[...] = jnp.zeros(gain_out.shape, F32)
+    for load in loads:
+        load.wait()
+
+    def run_tile(t):
+        slot = t % 2
+        rows_in[t].arrive()
+
+        def norm(i, carry):
+            first = t * rows + i * 32
+            at = pl.ds(pl.multiple_of(i * 32, 32), 32)
+            frame_rows = [
+                context[pl.ds(t * tile + i * 4 + f, 1)] for f in range(4)
+            ]
+            spread = jnp.concatenate([jnp.broadcast_to(row, (8, width)) for row in frame_rows], axis=0)
+            embedded = jnp.concatenate(
+                [e_in[j, pl.ds(pl.multiple_of(first, 32), 32)] for j in range(column_blocks)], axis=1
+            )
+            depth = (spread + embedded.astype(F32)).astype(BF16).astype(F32)
+            inv = lax.rsqrt(jnp.mean(depth * depth, axis=1, keepdims=True) + EPSILON)
+            unit_rows = depth * inv
+            unit[at] = unit_rows
+            scale[at] = jnp.broadcast_to(inv, (32, 128))
+            normed[slot, at] = (unit_rows * gain[...]).astype(BF16)
+            return carry
+
+        lax.fori_loop(0, rows // 32, norm, 0)
+
+        def forward_pass(j, carry):
+            columns = pl.ds(pl.multiple_of(j * 256, 256), 256)
+            left = normed[slot]
+            gate = jnp.dot(left, gate_w[:, columns], preferred_element_type=F32)
+            up = jnp.dot(left, up_w[:, columns], preferred_element_type=F32)
+            upstream = hidden_in[pl.ds(t * rows, rows), columns].astype(F32)
+            sigma = jax.nn.sigmoid(gate)
+            with_sigma = upstream * sigma
+            gate_back[slot, :, columns] = (with_sigma * up * (1.0 + gate * (1.0 - sigma))).astype(BF16)
+            up_back[slot, :, columns] = (with_sigma * gate).astype(BF16)
+            return carry
+
+        lax.fori_loop(0, gate_w.shape[1] // 256, forward_pass, 0)
+        outs = [
+            pltpu.make_async_copy(ref.at[slot], target.at[pl.ds(t * rows, rows)], out_sems.at[slot, n])
+            for n, (ref, target) in enumerate(
+                ((normed, normed_out), (gate_back, gate_out), (up_back, up_out))
+            )
+        ]
+        for out in outs:
+            out.start()
+
+        transposed = (((1,), (1,)), ((), ()))
+
+        def backward_pass(j, carry):
+            columns = pl.ds(pl.multiple_of(j * 256, 256), 256)
+            total = lax.dot_general(
+                gate_back[slot], gate_w[columns], transposed, preferred_element_type=F32
+            )
+            total = total + lax.dot_general(
+                up_back[slot], up_w[columns], transposed, preferred_element_type=F32
+            )
+            back[:, columns] = total
+            return carry
+
+        lax.fori_loop(0, width // 256, backward_pass, 0)
+
+        def finish(i, carry):
+            at = pl.ds(pl.multiple_of(i * 64, 64), 64)
+            whole = pl.ds(pl.multiple_of(t * rows + i * 64, 64), 64)
+            normed_back, unit_rows = back[at], unit[at]
+            gain_out[...] += jnp.sum((normed_back * unit_rows).reshape(8, 8, width), axis=0)
+            scaled = normed_back * gain[...]
+            mean = jnp.mean(scaled * unit_rows, axis=1, keepdims=True)
+            depth = stream_in[whole].astype(F32) + scale[at, :1] * (scaled - unit_rows * mean)
+            depth = depth.astype(BF16)
+            for j in range(column_blocks):
+                g_send[j, whole] = depth[:, j * 128 : (j + 1) * 128]
+            frame_rows = pl.ds(pl.multiple_of(t * tile + i * 8, 8), 8)
+            context_grad[frame_rows] = jnp.sum(depth.astype(F32).reshape(8, 8, width), axis=1)
+            return carry
+
+        lax.fori_loop(0, rows // 64, finish, 0)
+        for by_x, by_z in ORDER[:-1]:
+            rows_back[t].start(by_x, by_z)
+        grid_out[own, pl.ds(t * rows, rows)] = g_send[own, pl.ds(t * rows, rows)]
+        return outs
+
+    outs = [run_tile(0)]
+    rows_in[3].forward()
+    outs.append(run_tile(1))
+    rows_back[0].forward()
+    for out in outs[0]:
+        out.wait()
+    outs.append(run_tile(2))
+    rows_back[1].forward()
+    for out in outs[1]:
+        out.wait()
+    outs.append(run_tile(3))
+    rows_back[2].forward()
+    context_out[...] = context_grad[...].astype(BF16)
+    rows_back[3].forward()
+    for out in outs[2] + outs[3]:
+        out.wait()
+    for t in range(TILES):
+        rows_back[t].arrive()
+    copies.finish()
+
+
+def front(ids, text_table, code_tables, temporal, context_weight, gain, gate_weight, up_weight, hidden, stream):
+    frames_all = temporal.shape[0]
+    frames = frames_all // 8
+    width, hidden_width = gate_weight.shape
+    rows = frames * 8 // TILES
+    bf = lambda *shape: pltpu.VMEM(shape, BF16)
+    f32 = lambda *shape: pltpu.VMEM(shape, F32)
+    dma = lambda *shape: pltpu.SemaphoreType.DMA(shape)
+    vmem = pl.BlockSpec(memory_space=pltpu.VMEM)
+    anywhere = pl.BlockSpec(memory_space=pl.ANY)
+    table_rows = text_table.shape[0] + code_tables.shape[0]
+    return pl.pallas_call(
+        front_kernel,
+        out_shape=(
+            jax.ShapeDtypeStruct((frames * 8, width), BF16),
+            jax.ShapeDtypeStruct((frames * 8, hidden_width), BF16),
+            jax.ShapeDtypeStruct((frames * 8, hidden_width), BF16),
+            jax.ShapeDtypeStruct((8, width), F32),
+            jax.ShapeDtypeStruct((frames, width), BF16),
+            jax.ShapeDtypeStruct((8, frames * 8, 128), BF16),
+        ),
+        in_specs=[pl.BlockSpec(memory_space=pltpu.SMEM), anywhere, anywhere, vmem, vmem, vmem]
+        + [anywhere] * 4,
+        out_specs=(anywhere, anywhere, anywhere, vmem, vmem, vmem),
+        scratch_shapes=[
+            f32(table_rows, 128), bf(2, 2048, 128), dma(2), f32(rows, 128),
+            bf(4, 2, frames, width), bf(2, frames, width), bf(2, frames, width), bf(2, frames, width),
+            bf(2, frames, width), bf(frames, width), f32(frames, width),
+            bf(8, frames * 8, 128), bf(8, frames * 8, 128), bf(TILES, 2, 2, rows // 2, 128),
+            bf(8, frames * 8, 128), bf(TILES, 2, 2, rows // 2, 128),
+            bf(width, hidden_width), bf(width, hidden_width),
+            bf(frames * 8, hidden_width), bf(frames * 8, width), dma(4),
+            bf(2, rows, width), bf(2, rows, hidden_width), bf(2, rows, hidden_width), dma(2, 3),
+            f32(rows, width), f32(rows, 128), f32(rows, width), f32(frames, width),
+            dma(120), dma(120),
+        ],
+        compiler_params=pltpu.CompilerParams(
+            collective_id=2, has_side_effects=True, vmem_limit_bytes=VMEM_LIMIT
+        ),
+        cost_estimate=pl.CostEstimate(
+            flops=19_000_000_000, bytes_accessed=40_000_000, transcendentals=2_000_000
+        ),
+        name="front",
+    )(ids, text_table, code_tables, temporal, context_weight, gain, gate_weight, up_weight, hidden, stream)
 
 
 def reduce_kernel(
@@ -473,56 +794,24 @@
     hidden_grad,
     stream_grad,
 ):
-    code_count = code_tables.shape[0]
-    card_size = code_tables.shape[1]
-    own_frames = hidden_grad.shape[0]
-    step_count = hidden_grad.shape[1]
-    model_width = gate_weight.shape[0]
-    hidden_width = gate_weight.shape[1]
-    code_offsets = jnp.arange(code_count, dtype=jnp.int32)[None, :] * card_size
-    text_rows = jnp.take(text_table, text_ids, axis=0)
-    code_rows = jnp.take(
-        code_tables.reshape(code_count * card_size, -1), code_ids + code_offsets, axis=0
+    code_count, card_size, feature_width = code_tables.shape
+    text_count = text_table.shape[0]
+    code_offsets = jnp.arange(code_count, dtype=jnp.int32)[:, None] * card_size + text_count
+    places = jnp.concatenate([text_ids[None], code_ids.T + code_offsets], axis=0).reshape(-1)
+    normed, gate_back, up_back, gain_part, context_grad, grid = front(
+        places,
+        text_table,
+        code_tables.reshape(code_count * card_size, feature_width),
+        temporal_out,
+        context_weight,
+        norm_gain.reshape(1, -1),
+        gate_weight,
+        up_weight,
+        hidden_grad.reshape(-1, hidden_grad.shape[2]),
+        stream_grad.reshape(-1, stream_grad.shape[2]),
     )
-    embedded = jnp.concatenate([text_rows[:, None, :], code_rows], axis=1)
-    partial_value = jnp.dot(temporal_out, context_weight, preferred_element_type=jnp.float32)
-    context_slice = lax.psum_scatter(
-        partial_value.astype(jnp.bfloat16), "tp", scatter_dimension=1, tiled=True
-    ).astype(jnp.float32)
-    feature_rows = (context_slice[:, None, :] + embedded.astype(jnp.float32)).astype(jnp.bfloat16)
-    depth_in = lax.all_to_all(feature_rows, "tp", split_axis=0, concat_axis=2, tiled=True)
-    depth_rows = depth_in.reshape(-1, model_width).astype(jnp.float32)
-    inv_rms = lax.rsqrt(jnp.mean(depth_rows * depth_rows, axis=1, keepdims=True) + EPSILON)
-    unit_rows = depth_rows * inv_rms
-    normed = (unit_rows * norm_gain).astype(jnp.bfloat16)
-    gate_values = jnp.dot(normed, gate_weight, preferred_element_type=jnp.float32)
-    up_values = jnp.dot(normed, up_weight, preferred_element_type=jnp.float32)
-    gate_sigmoid = jax.nn.sigmoid(gate_values)
-    upstream = hidden_grad.reshape(-1, hidden_width).astype(jnp.float32)
-    gate_back = (
-        upstream * up_values * gate_sigmoid * (1.0 + gate_values * (1.0 - gate_sigmoid))
-    ).astype(jnp.bfloat16)
-    up_back = (upstream * gate_values * gate_sigmoid).astype(jnp.bfloat16)
-    transposed = (((1,), (1,)), ((), ()))
-    normed_back = lax.dot_general(
-        gate_back, gate_weight, transposed, preferred_element_type=jnp.float32
-    )
-    normed_back = normed_back + lax.dot_general(
-        up_back, up_weight, transposed, preferred_element_type=jnp.float32
-    )
-    gain_part = jnp.sum(normed_back * unit_rows, axis=0)
-    scaled_back = normed_back * norm_gain
-    stream_rows = stream_grad.reshape(-1, model_width).astype(jnp.float32)
-    depth_back = stream_rows + inv_rms * (
-        scaled_back - unit_rows * jnp.mean(scaled_back * unit_rows, axis=1, keepdims=True)
-    )
-    depth_grid = depth_back.astype(jnp.bfloat16).reshape(own_frames, step_count, model_width)
-    context_grad = jnp.sum(depth_grid.astype(jnp.float32), axis=1).astype(jnp.bfloat16)
-    feature_grid = lax.all_to_all(depth_grid, "tp", split_axis=2, concat_axis=0, tiled=True)
-    places = jnp.concatenate(
-        [text_ids[None], code_ids.T + code_offsets.T + text_table.shape[0]], axis=0
-    ).reshape(-1)
-    tables = scatter_rows(places, feature_grid, text_table.shape[0], card_size, code_count)
+    gain_part = jnp.sum(gain_part, axis=0)
+    tables = scatter_rows(places, grid.reshape(-1, 8, feature_width), text_count, card_size, code_count)
     gate_grad, up_grad, gain_sum, text_grad, code_sum = reduce_all(
         normed, gate_back, up_back, gain_part, tables
     )

time: 304 us -> 216 us (0.71)
  Pallas kernels: 102 us -> 203 us
  waiting for transfers between devices: 46.6 us -> 0 us
  local copies, waits for them, and re-layouts: 53.4 us -> 9.22 us
  matrix products: 37.8 us -> 0 us
  blocking collectives: 31.1 us -> 0 us
  between operations: 14.3 us -> 0.67 us
  other arithmetic: 12.6 us -> 2.9 us
  starting transfers between devices: 3.64 us -> 0 us
    pallas_call x0 -> x1, Pallas kernels: none -> 98.1 us  [front(): pl.pallas_call(front_kernel, out_shape=(jax.ShapeDtypeStruct((frames * 8,...]
    dot_general x5 -> x0, matrix products: 37.8 us -> none  [the longest x1 11.6 us: on_device(): up_values = jnp.dot(normed, up_weight, preferred_element_type=jnp.float32)]
    all_to_all x1 -> x0, blocking collectives: 31.1 us -> none  [on_device(): lax.all_to_all(feature_rows, 'tp', split_axis=0, concat_axis=2, tiled=True)]
    gather x3 -> x0, local copies, waits for them, and re-layouts: 29.1 us -> none  [the longest x2 23.3 us: on_device(): jnp.take(code_tables.reshape(code_count * card_size, -1), code_ids + code...]
    all_to_all x1 -> x0, waiting for transfers between devices: 28 us -> none  [on_device(): lax.all_to_all(depth_grid, 'tp', split_axis=2, concat_axis=0, tiled=True)]
    unnamed x2 -> x0, waiting for transfers between devices: 18.7 us -> none
    unnamed x31 -> x8, local copies, waits for them, and re-layouts: 15 us -> 7.95 us
    select_n x2 -> x0, other arithmetic: 4.55 us -> none  [the longest x1 4.34 us: on_device(): jnp.take(code_tables.reshape(code_count * card_size, -1), code_ids + code...]
  transfers between devices with their start and end apart: 2 -> 0, of which waited for: 2 -> 0; matrix products, arithmetic and copies ran while one was open for 12% -> 0% of each run, Pallas kernels for 0% -> 0%
where the time goes in v2:
time: 216 us
  Pallas kernels  203 us (94%)
  local copies, waits for them, and re-layouts  9.22 us (4%)
  other arithmetic  2.9 us (1%)
    pallas_call x1, Pallas kernels, front(): pl.pallas_call(front_kernel, out_shape=(jax.ShapeDtypeStruct((frames * 8,...  98.1 us
    pallas_call x1, Pallas kernels, reduce_all(): pl.pallas_call(reduce_kernel, out_shape=(jax.ShapeDtypeStruct((out_rows,...  86.1 us
    pallas_call x1, Pallas kernels, scatter_rows(): pl.pallas_call(functools.partial(scatter_kernel, text_count=text_count, c...  18.8 us
    unnamed x8, local copies, waits for them, and re-layouts  7.95 us

profile of v2, /device:TPU:0, one launch (start us, length us, event | category | flops | bytes accessed | tf_op | source)
XLA Modules:
  0.0 215.8 jit_solution(9970101769521139775)
XLA Ops:
  0.6 0.8 add_bitcast_fusion.1
  1.5 0.7 add_bitcast_fusion
  2.2 0.6 copy.19
  2.8 98.1 %front.1 = (bf16[1024,1024]{1,0:T(8,128)(2,1)}, bf16[1024,2048]{1,0:T(8,128)(2,1)}, bf16[1024,2048]{1,0:T(8,128)(2,1)}, f32[8,1024]{1,0:T(8,128)}, bf16[128,1024...) custom-call(s32[8192]{0:T(1024)} %bitcast.18, bf16[16384,128]{1,0:T(8,128)(2,1)} %text_table.1, bf16[14336,128]{1,0:T(8,128)(2,1)} %bitcast.23, ...), custom_call_target="tpu_custom_call" | custom-call | flops 19000000512 | bytes 40000000 | tf_op jit(solution)/shard_map/front/pallas_call | solution.py:400
  100.9 1.4 reduce_sum.9
  102.3 18.8 %scatter_rows.1.tables = bf16[2,4,2,1920,128]{4,3,2,1,0:T(8,128)(2,1)} custom-call(s32[8192]{0:T(1024)} %bitcast.19, bf16[1024,8,128]{2,1,0:T(8,128)(2,1)} %bitcast.16), custom_call_target="tpu_custom_call" | custom-call | tf_op jit(solution)/shard_map/scatter_rows/pallas_call | solution.py:770
  121.1 0.0 copy-start
  121.1 86.1 %reduce_all.1 = (f32[8,2048]{1,0:T(8,128)}, f32[8,2048]{1,0:T(8,128)}, f32[8,128]{1,0:T(8,128)}, f32[1024,128]{1,0:T(8,128)}, f32[896,128]{1,0:T(8,128)}) custom-call(bf16[1024,1024]{1,0:T(8,128)(2,1)} %get-tuple-element.17.normed, bf16[1024,2048]{1,0:T(8,128)(2,1)} %get-tuple-element.18.gate_back, bf16[1024,2048]{1,0:T(8,128)(2,1)} %get-tuple-element.19.up_back, ...), custom_call_target="tpu_custom_call" | custom-call | flops 8999999488 | bytes 20000000 | tf_op jit(solution)/shard_map/reduce_all/pallas_call | solution.py:692
  207.2 1.3 dynamic_slice.3
  208.4 1.5 copy.25
  209.9 1.5 copy.26
  211.4 1.9 copy.27
  213.3 1.8 copy.28
  215.1 0.0 copy-done
  215.1 0.7 copy.29
  (1 shorter events, 0.0 us)
Async XLA Ops:
  121.1 94.0 %copy-start = (bf16[128,1024]{1,0:T(8,128)(2,1)S(1)}, bf16[128,1024]{1,0:T(8,128)(2,1)}, u32[]{:S(2)}) copy-start(bf16[128,1024]{1,0:T(8,128)(2,1)} %get-tuple-element.39) | copy-start | bytes 786436

commit v3 on v2

--- a/solution.py
+++ b/solution.py
@@ -144,7 +144,7 @@
     c_term, c_pass, c_direct, c_ended, c_pair, c_last, context,
     e_send, e_in, e_relay, g_send, g_relay,
     gate_w, up_w, hidden_in, stream_in, load_sems,
-    normed, gate_back, up_back, out_sems, unit, scale, back, context_grad, send_sems, recv_sems,
+    normed, gate_back, up_back, out_sems, unit, scale, back, context_grad, gain_sum, send_sems, recv_sems,
 ):
     core, x, y, z = position()
     z_lo = lax.rem(z, 2)
@@ -279,7 +279,7 @@
 
     width = context.shape[1]
     column_blocks = width // 128
-    gain_out[...] = jnp.zeros(gain_out.shape, F32)
+    gain_sum[...] = jnp.zeros(gain_sum.shape, F32)
     for load in loads:
         load.wait()
 
@@ -348,7 +348,7 @@
             at = pl.ds(pl.multiple_of(i * 64, 64), 64)
             whole = pl.ds(pl.multiple_of(t * rows + i * 64, 64), 64)
             normed_back, unit_rows = back[at], unit[at]
-            gain_out[...] += jnp.sum((normed_back * unit_rows).reshape(8, 8, width), axis=0)
+            gain_sum[...] += jnp.sum((normed_back * unit_rows).reshape(8, 8, width), axis=0)
             scaled = normed_back * gain[...]
             mean = jnp.mean(scaled * unit_rows, axis=1, keepdims=True)
             depth = stream_in[whole].astype(F32) + scale[at, :1] * (scaled - unit_rows * mean)
@@ -378,6 +378,9 @@
     outs.append(run_tile(3))
     rows_back[2].forward()
     context_out[...] = context_grad[...].astype(BF16)
+    gain_row = jnp.sum(gain_sum[...], axis=0, keepdims=True)
+    for j in range(8):
+        gain_out[j : j + 1] = gain_row[:, j * 128 : (j + 1) * 128]
     rows_back[3].forward()
     for out in outs[2] + outs[3]:
         out.wait()
@@ -403,7 +406,7 @@
             jax.ShapeDtypeStruct((frames * 8, width), BF16),
             jax.ShapeDtypeStruct((frames * 8, hidden_width), BF16),
             jax.ShapeDtypeStruct((frames * 8, hidden_width), BF16),
-            jax.ShapeDtypeStruct((8, width), F32),
+            jax.ShapeDtypeStruct((8, width // 8), F32),
             jax.ShapeDtypeStruct((frames, width), BF16),
             jax.ShapeDtypeStruct((8, frames * 8, 128), BF16),
         ),
@@ -419,7 +422,7 @@
             bf(width, hidden_width), bf(width, hidden_width),
             bf(frames * 8, hidden_width), bf(frames * 8, width), dma(4),
             bf(2, rows, width), bf(2, rows, hidden_width), bf(2, rows, hidden_width), dma(2, 3),
-            f32(rows, width), f32(rows, 128), f32(rows, width), f32(frames, width),
+            f32(rows, width), f32(rows, 128), f32(rows, width), f32(frames, width), f32(8, width),
             dma(120), dma(120),
         ],
         compiler_params=pltpu.CompilerParams(
@@ -432,23 +435,51 @@
     )(ids, text_table, code_tables, temporal, context_weight, gain, gate_weight, up_weight, hidden, stream)
 
 
+CHUNKS = 3
+
+
+def total_of(refs):
+    total = refs[0][...].astype(F32)
+    for ref in refs[1:]:
+        total = total + ref[...].astype(F32)
+    return total
+
+
+def add_into(out, refs):
+    out[...] = total_of(refs).astype(BF16)
+
+
 def reduce_kernel(
     normed, gate_back, up_back, gain, tables,
-    gate_out, up_out, gain_out, text_out, code_out,
-    turned, term, pair, x_pass, x_direct, x_ended, z_term, z_pass, z_direct, z_ended,
-    y_term, y_pass, y_direct, y_ended, own, other, t_pass, t_direct, t_ended, t_sum, t_last,
-    gain_own, gain_in, local_sem, send_sems, recv_sems,
+    weight_out, gain_out, table_mine, table_last,
+    left_in, gate_in, up_in, turned, term, pair,
+    x_bufs, x_sums, xz_bufs, z_bufs, z_sums, zx_bufs, y_term, y_bufs,
+    own, other, t_bufs, t_sum, t_relay, gain_own, gain_in,
+    local_sems, send_sems, recv_sems,
 ):
     core, x, y, z = position()
-    half_width = term.shape[-1] // 2
-    text_rows = text_out.shape[0]
+    quarter = term.shape[-1] // 4
     table_rows = own.shape[2]
-    half_rows = table_rows // 2
+    chunk_rows = table_rows // CHUNKS
+    half_rows = chunk_rows // 2
     z_hi = lax.div(z, 2)
     sibling = device_at(1 - core, x, y, z)
     x_device = lambda at: device_at(core, at, y, z)
     y_device = lambda at: device_at(core, x, at, z)
     z_device = lambda at: device_at(core, x, y, at)
+    t_rows = lambda c: pl.ds(c * chunk_rows, chunk_rows)
+    keeps = [
+        pltpu.make_async_copy(tables.at[core, :, :, t_rows(c)], own.at[:, :, t_rows(c)], local_sems.at[c])
+        for c in range(CHUNKS)
+    ]
+    loads = [
+        pltpu.make_async_copy(source, target, local_sems.at[CHUNKS + n])
+        for n, (source, target) in enumerate(
+            ((normed, left_in), (gate_back, gate_in), (up_back, up_in))
+        )
+    ]
+    for load in loads + keeps:
+        load.start()
     greet(
         [sibling]
         + [x_device(step_to(x, by)) for by in (1, 2, 3)]
@@ -456,120 +487,146 @@
         + [z_device(step_to(z, by)) for by in (1, 2, 3)]
     )
     copies = Copies(send_sems, recv_sems)
-    halves = lambda half: pl.ds(half * half_width, half_width)
-
-    keep = pltpu.make_async_copy(tables.at[core], own, local_sem)
-    keep.start()
+
     table_pairs = [
-        copies.send(tables.at[1 - core, i], other.at[i], sibling) for i in range(4)
+        [
+            copies.send(tables.at[1 - core, i, :, t_rows(c)], other.at[i, :, t_rows(c)], sibling)
+            for i in range(4)
+        ]
+        for c in range(CHUNKS)
     ]
     gain_own[0] = gain[...]
     gain_copy = copies.send(gain_own.at[0], gain_in.at[0], sibling)
 
     def make_term(q):
-        turned[...] = normed[:, q * 256 : (q + 1) * 256].T
+        turned[:128] = left_in[:, q * 128 : (q + 1) * 128].T
+        turned[128:] = left_in[:, (q + 4) * 128 : (q + 5) * 128].T
 
         def body(i, carry):
             columns = pl.ds(pl.multiple_of(i * 256, 256), 256)
             left = turned[...]
-            gate = jnp.dot(left, gate_back[:, columns], preferred_element_type=F32)
-            up = jnp.dot(left, up_back[:, columns], preferred_element_type=F32)
+            gate = jnp.dot(left, gate_in[:, columns], preferred_element_type=F32)
+            up = jnp.dot(left, up_in[:, columns], preferred_element_type=F32)
             both = jnp.concatenate([gate.reshape(32, 8, 256), up.reshape(32, 8, 256)], axis=1)
             both = both.astype(BF16).reshape(2, 2, 4, 2, 16, 256)
-            for low in range(2):
-                term[:, :, q * 2 + low, :, :, columns] = both[low]
-            return carry
-
-        lax.fori_loop(0, gate_back.shape[1] // 256, body, 0)
+            for hi in range(2):
+                term[:, q, :, pl.ds(hi * 2, 2), :, columns] = both[hi]
+            return carry
+
+        lax.fori_loop(0, gate_in.shape[1] // 256, body, 0)
 
     pair_copies = []
 
     def send_pair(q):
-        rows = pl.ds(q * 2, 2)
-        pair_copies.append(copies.send(term.at[1 - core, :, rows], pair.at[:, rows], sibling))
+        pair_copies.append(copies.send(term.at[1 - core, q], pair.at[q], sibling))
 
     def add_pair(q):
         pair_copies[q].wait_recv()
 
         def body(i, carry):
-            column, rest = lax.div(i, 4), lax.rem(i, 4)
-            row, low = q * 2 + lax.div(rest, 2), lax.rem(rest, 2)
-            here = term[core, column, row, low].astype(F32)
-            term[core, column, row, low] = (here + pair[column, row, low].astype(F32)).astype(BF16)
+            column, depth = lax.div(i, 4), lax.rem(i, 4)
+            total = term[core, q, column, depth].astype(F32) + pair[q, column, depth].astype(F32)
+            term[core, q, column, depth] = total.astype(BF16)
             return carry
 
         lax.fori_loop(0, 16, body, 0)
 
-    def add_four(out, refs):
-        def body(i, carry):
-            row, low = lax.div(i, 2), lax.rem(i, 2)
-            total = refs[0][row, low].astype(F32)
-            for ref in refs[1:]:
-                total = total + ref[row, low].astype(F32)
-            out[row, low] = total.astype(BF16)
-            return carry
-
-        lax.fori_loop(0, 4, body, 0)
-
-    def x_ring(q):
-        rows = pl.ds(q * 2, 2)
-        pick = lambda ref: lambda half: ref.at[rows, :, :, halves(half)]
-        return Ring(
-            copies, x, x_device,
-            lambda at, half: term.at[core, at, rows, :, :, halves(half)],
-            pick(x_pass), pick(x_direct), pick(x_ended),
+    x_half = lambda half: pl.ds(half * quarter, quarter)
+    z_half = lambda half: pl.ds((half + 2) * quarter, quarter)
+
+    def make_ring(here, device, part, bufs, q):
+        picks = [
+            lambda half, n=n: bufs.at[(n, q) + (slice(None),) * (len(bufs.shape) - 3) + (x_half(half),)]
+            for n in range(3)
+        ]
+        return Ring(copies, here, device, part, *picks)
+
+    first_rings = [
+        (
+            make_ring(x, x_device, lambda at, half, q=q: term.at[core, q, at, :, :, x_half(half)], x_bufs, q),
+            make_ring(z, z_device, lambda at, half, q=q: term.at[core, q, :, at, :, z_half(half)], z_bufs, q),
         )
-
-    x_rings = [x_ring(q) for q in range(4)]
-
-    def x_out(q):
-        def finish(out, refs):
-            def body(i, carry):
-                row, low = lax.div(i, 2), lax.rem(i, 2)
-                total = refs[0][row, low].astype(F32)
-                for ref in refs[1:]:
-                    total = total + ref[row, low].astype(F32)
-                z_term[q // 2 * 2 + low, q % 2 * 2 + row, :, out] = total.astype(BF16)
-                return carry
-
-            lax.fori_loop(0, 4, body, 0)
-
-        x_rings[q].third(finish, halves)
-
-    t_half = lambda half: pl.ds(half * half_rows, half_rows)
-    t_pick = lambda ref: lambda half: ref.at[:, t_half(half)]
-    t_ring = Ring(
-        copies, y, y_device,
-        lambda at, half: own.at[at, :, t_half(half)],
-        t_pick(t_pass), t_pick(t_direct), t_pick(t_ended),
-    )
+        for q in range(4)
+    ]
+    second_rings = [
+        (
+            make_ring(z, z_device, lambda at, half, q=q: x_sums.at[q, at, :, x_half(half)], xz_bufs, q),
+            make_ring(x, x_device, lambda at, half, q=q: z_sums.at[q, at, :, x_half(half)], zx_bufs, q),
+        )
+        for q in range(4)
+    ]
+
+    def first_out(q):
+        first_rings[q][0].third(add_into, lambda half: x_sums.at[q, :, :, x_half(half)])
+        first_rings[q][1].third(add_into, lambda half: z_sums.at[q, :, :, x_half(half)])
+        for ring in second_rings[q]:
+            ring.first()
+
+    def second_out(q):
+        second_rings[q][0].third(add_into, lambda half: y_term.at[q, :, x_half(half)])
+        second_rings[q][1].third(add_into, lambda half: y_term.at[q, :, z_half(half)])
+
+    def first_start(q):
+        add_pair(q)
+        for ring in first_rings[q]:
+            ring.first()
+
+    def first_middle(q):
+        for ring in first_rings[q]:
+            ring.second(add_into)
+
+    def second_middle(q):
+        for ring in second_rings[q]:
+            ring.second(add_into)
+
+    t_half = lambda c, half: pl.ds(c * chunk_rows + half * half_rows, half_rows)
+    t_rings = [
+        Ring(
+            copies, y, y_device,
+            lambda at, half, c=c: own.at[at, :, t_half(c, half)],
+            *(lambda half, n=n, c=c: t_bufs.at[n, :, t_half(c, half)] for n in range(3)),
+        )
+        for c in range(CHUNKS)
+    ]
 
     def add_tables(out, refs):
         def body(i, carry):
             rows = pl.ds(pl.multiple_of(i * 64, 64), 64)
             for hi in range(2):
-                total = refs[0][hi, rows].astype(F32)
-                for ref in refs[1:]:
-                    total = total + ref[hi, rows].astype(F32)
-                out[hi, rows] = total.astype(BF16)
+                out[hi, rows] = total_of([ref.at[hi, rows] for ref in refs]).astype(BF16)
             return carry
 
         lax.fori_loop(0, half_rows // 64, body, 0)
 
-    def pair_tables():
-        keep.wait()
-        for copy in table_pairs:
+    def pair_tables(c):
+        keeps[c].wait()
+        for copy in table_pairs[c]:
             copy.wait_recv()
 
         def body(i, carry):
-            rows = pl.ds(pl.multiple_of(lax.rem(i, table_rows // 64) * 64, 64), 64)
-            at = lax.div(i, table_rows // 64)
+            rows = pl.ds(pl.multiple_of(c * chunk_rows + lax.rem(i, chunk_rows // 128) * 128, 128), 128)
+            at = lax.div(i, chunk_rows // 128)
             for hi in range(2):
-                total = own[at, hi, rows].astype(F32) + other[at, hi, rows].astype(F32)
-                own[at, hi, rows] = total.astype(BF16)
-            return carry
-
-        lax.fori_loop(0, 4 * table_rows // 64, body, 0)
+                own[at, hi, rows] = total_of([own.at[at, hi, rows], other.at[at, hi, rows]]).astype(BF16)
+            return carry
+
+        lax.fori_loop(0, 4 * (chunk_rows // 128), body, 0)
+        t_rings[c].first()
+
+    t_relays, t_arrivals = {}, []
+
+    def tables_out(c):
+        t_rings[c].third(add_tables, lambda half: t_sum.at[:, t_half(c, half)])
+        t_relays[c] = [
+            copies.send(t_sum.at[1 - z_hi, t_half(c, half)], t_relay.at[t_half(c, half)], z_device(step_to(z, by)))
+            for half, by in ((0, 1), (1, 3))
+        ]
+
+    def tables_relay(c):
+        for copy, half, by in zip(t_relays[c], (0, 1), (1, 3)):
+            copy.wait_recv()
+            rows = t_half(c, half)
+            t_arrivals.append(copies.send(t_relay.at[rows], table_last.at[rows], z_device(step_to(z, by))))
 
     def gain_round(index, device, here):
         gain_own[index] = gain_own[index - 1] + gain_sum
@@ -586,141 +643,151 @@
             total = total + gain_in[slot]
         return total
 
+    for load in loads:
+        load.wait()
     make_term(0)
     send_pair(0)
-    pair_tables()
-    t_ring.first()
+    pair_tables(0)
+    pair_tables(1)
     make_term(1)
     send_pair(1)
-    add_pair(0)
-    x_rings[0].first()
+    pair_tables(2)
+    first_start(0)
+    t_rings[0].second(add_tables)
     gain_sum = gain_total([gain_copy], [0])
     gain_copies = gain_round(1, x_device, x)
     make_term(2)
     send_pair(2)
-    add_pair(1)
-    x_rings[1].first()
-    t_ring.second(add_tables)
+    first_start(1)
+    first_middle(0)
+    t_rings[1].second(add_tables)
     make_term(3)
     send_pair(3)
-    add_pair(2)
-    x_rings[2].first()
-    x_rings[0].second(add_four)
-    add_pair(3)
-    x_rings[3].first()
-    x_rings[1].second(add_four)
+    first_start(2)
+    first_middle(1)
+    first_out(0)
     gain_sum = gain_total(gain_copies, [1, 2, 3])
     gain_copies = gain_round(2, y_device, y)
-    x_out(0)
-    x_rings[2].second(add_four)
-    x_out(1)
-    t_ring.third(add_tables, lambda half: t_sum.at[:, t_half(half)])
-    t_copy = copies.send(t_sum.at[1 - z_hi], t_last, z_device(step_to(z, 2)))
-    x_rings[3].second(add_four)
-    x_out(2)
+    first_start(3)
+    first_middle(2)
+    first_out(1)
+    second_middle(0)
+    t_rings[2].second(add_tables)
+    tables_out(0)
+    first_middle(3)
+    first_out(2)
+    second_middle(1)
+    second_out(0)
+    tables_out(1)
+    tables_relay(0)
     gain_sum = gain_total(gain_copies, [4, 5, 6])
     gain_copies = gain_round(3, z_device, z)
-    x_out(3)
-
-    def add_few(out, refs):
-        for i in range(4):
-            total = refs[0][i].astype(F32)
-            for ref in refs[1:]:
-                total = total + ref[i].astype(F32)
-            out[i] = total.astype(BF16)
-
-    z_pick = lambda ref: lambda half: ref.at[:, :, halves(half)]
-    z_ring = Ring(
-        copies, z, z_device,
-        lambda at, half: z_term.at[at, :, :, halves(half)],
-        z_pick(z_pass), z_pick(z_direct), z_pick(z_ended),
-    )
-    z_ring.first()
-    z_ring.second(add_few)
-    z_ring.third(add_few, lambda half: y_term.at[:, :, halves(half)])
-
-    def add_one(out, refs):
-        total = refs[0][...].astype(F32)
-        for ref in refs[1:]:
-            total = total + ref[...].astype(F32)
-        out[...] = total.astype(BF16)
-
-    y_pick = lambda ref: lambda half: ref.at[:, halves(half)]
+    first_out(3)
+    second_middle(2)
+    second_out(1)
+    tables_relay(1)
+    tables_out(2)
+    second_middle(3)
+    second_out(2)
+    second_out(3)
+
+    y_half = lambda half: pl.ds(half * 2 * quarter, 2 * quarter)
     y_ring = Ring(
         copies, y, y_device,
-        lambda at, half: y_term.at[at, :, halves(half)],
-        y_pick(y_pass), y_pick(y_direct), y_pick(y_ended),
+        lambda at, half: y_term.at[at, :, y_half(half)],
+        *(lambda half, n=n: y_bufs.at[n, :, y_half(half)] for n in range(3)),
     )
     y_ring.first()
-    t_copy.wait_recv()
-
-    def text_body(i, carry):
-        rows = pl.ds(pl.multiple_of(i * 64, 64), 64)
-        text_out[rows] = t_sum[z_hi, rows].astype(F32) + t_last[rows].astype(F32)
+    tables_relay(2)
+    gain_out[...] = gain_own[3] + gain_total(gain_copies, [7, 8, 9])
+    y_ring.second(add_into)
+
+    def copy_mine(i, carry):
+        rows = pl.ds(pl.multiple_of(i * 128, 128), 128)
+        table_mine[rows] = t_sum[z_hi, rows]
         return carry
 
-    lax.fori_loop(0, text_rows // 64, text_body, 0)
-
-    def code_body(i, carry):
-        at = pl.ds(pl.multiple_of(i * 64, 64), 64)
-        rows = pl.ds(pl.multiple_of(text_rows + i * 64, 64), 64)
-        code_out[at] = t_sum[z_hi, rows].astype(F32) + t_last[rows].astype(F32)
-        return carry
-
-    lax.fori_loop(0, code_out.shape[0] // 64, code_body, 0)
-    gain_out[...] = gain_own[3] + gain_total(gain_copies, [7, 8, 9])
-    y_ring.second(add_one)
+    lax.fori_loop(0, table_rows // 128, copy_mine, 0)
 
     def finish_weights(out, refs):
-        total = refs[0][...].astype(F32)
-        for ref in refs[1:]:
-            total = total + ref[...].astype(F32)
-        gate_out[:, out] = total[:8]
-        up_out[:, out] = total[8:]
-
-    y_ring.third(finish_weights, halves)
+        weight_out[:, out] = total_of(refs)
+
+    y_ring.third(finish_weights, y_half)
+    for copy in t_arrivals:
+        copy.wait_recv()
     copies.finish()
 
 
 def reduce_all(normed, gate_back, up_back, gain_part, tables):
-    features, width = normed.shape[1], gate_back.shape[1]
+    rows, features = normed.shape
+    width = gate_back.shape[1]
     table_rows = tables.shape[3]
-    text_rows = table_rows * 8 // 15
-    out_rows = features // 128
     bf = lambda *shape: pltpu.VMEM(shape, BF16)
     vmem = pl.BlockSpec(memory_space=pltpu.VMEM)
+    anywhere = pl.BlockSpec(memory_space=pl.ANY)
     return pl.pallas_call(
         reduce_kernel,
         out_shape=(
-            jax.ShapeDtypeStruct((out_rows, width), F32),
-            jax.ShapeDtypeStruct((out_rows, width), F32),
+            jax.ShapeDtypeStruct((16, width), F32),
             jax.ShapeDtypeStruct((8, 128), F32),
-            jax.ShapeDtypeStruct((text_rows, 128), F32),
-            jax.ShapeDtypeStruct((table_rows - text_rows, 128), F32),
+            jax.ShapeDtypeStruct((table_rows, 128), BF16),
+            jax.ShapeDtypeStruct((table_rows, 128), BF16),
         ),
-        in_specs=[vmem] * 4 + [pl.BlockSpec(memory_space=pl.ANY)],
-        out_specs=(vmem,) * 5,
+        in_specs=[anywhere, anywhere, anywhere, vmem, anywhere],
+        out_specs=(vmem,) * 4,
         scratch_shapes=[
-            bf(256, normed.shape[0]),
-            bf(2, 4, 8, 2, 16, width),
-            bf(4, 8, 2, 16, width),
-            bf(8, 2, 16, width), bf(8, 2, 16, width), bf(8, 2, 16, width),
-            bf(4, 4, 16, width), bf(4, 16, width), bf(4, 16, width), bf(4, 16, width),
-            bf(4, 16, width), bf(16, width), bf(16, width), bf(16, width),
-            bf(4, 2, table_rows, 128), bf(4, 2, table_rows, 128),
-            bf(2, table_rows, 128), bf(2, table_rows, 128), bf(2, table_rows, 128),
+            bf(rows, features), bf(rows, width), bf(rows, width), bf(256, rows),
+            bf(2, 4, 4, 4, 16, width), bf(4, 4, 4, 16, width),
+            bf(3, 4, 4, 16, width // 2), bf(4, 4, 16, width // 2), bf(3, 4, 16, width // 2),
+            bf(3, 4, 4, 16, width // 2), bf(4, 4, 16, width // 2), bf(3, 4, 16, width // 2),
+            bf(4, 16, width), bf(3, 16, width),
+            bf(4, 2, table_rows, 128), bf(4, 2, table_rows, 128), bf(3, 2, table_rows, 128),
             bf(2, table_rows, 128), bf(table_rows, 128),
             pltpu.VMEM((4, 8, 128), F32), pltpu.VMEM((10, 8, 128), F32),
-            pltpu.SemaphoreType.DMA,
-            pltpu.SemaphoreType.DMA((64,)),
-            pltpu.SemaphoreType.DMA((64,)),
+            pltpu.SemaphoreType.DMA((CHUNKS + 3,)),
+            pltpu.SemaphoreType.DMA((160,)),
+            pltpu.SemaphoreType.DMA((160,)),
         ],
         compiler_params=pltpu.CompilerParams(
             collective_id=1, has_side_effects=True, vmem_limit_bytes=VMEM_LIMIT
         ),
         cost_estimate=pl.CostEstimate(flops=9_000_000_000, bytes_accessed=20_000_000, transcendentals=0),
         name="reduce_all",
-    )(normed, gate_back, up_back, gain_part.reshape(8, 128), tables)
+    )(normed, gate_back, up_back, gain_part, tables)
+
+
+def results_kernel(weights, mine, last, gate_out, up_out, text_out, code_out):
+    gate_out[...] = weights[:8]
+    up_out[...] = weights[8:]
+    text_rows = text_out.shape[0]
+
+    def text_body(i, carry):
+        rows = pl.ds(pl.multiple_of(i * 128, 128), 128)
+        text_out[rows] = mine[rows].astype(F32) + last[rows].astype(F32)
+        return carry
+
+    lax.fori_loop(0, text_rows // 128, text_body, 0)
+    for c in range(code_out.shape[0]):
+        rows = pl.ds(text_rows + c * code_out.shape[1], code_out.shape[1])
+        code_out[c] = mine[rows].astype(F32) + last[rows].astype(F32)
+
+
+def results(weights, mine, last, text_rows, codes):
+    vmem = pl.BlockSpec(memory_space=pltpu.VMEM)
+    code_rows = (mine.shape[0] - text_rows) // codes
+    return pl.pallas_call(
+        results_kernel,
+        out_shape=(
+            jax.ShapeDtypeStruct((8, weights.shape[1]), F32),
+            jax.ShapeDtypeStruct((8, weights.shape[1]), F32),
+            jax.ShapeDtypeStruct((text_rows, 128), F32),
+            jax.ShapeDtypeStruct((codes, code_rows, 128), F32),
+        ),
+        in_specs=[vmem] * 3,
+        out_specs=(vmem,) * 4,
+        compiler_params=pltpu.CompilerParams(vmem_limit_bytes=VMEM_LIMIT),
+        name="results",
+    )(weights, mine, last)
 
 
 def scatter_kernel(ids, grads, tables, rows, total, text_count, card, codes):
@@ -810,14 +877,13 @@
         hidden_grad.reshape(-1, hidden_grad.shape[2]),
         stream_grad.reshape(-1, stream_grad.shape[2]),
     )
-    gain_part = jnp.sum(gain_part, axis=0)
     tables = scatter_rows(places, grid.reshape(-1, 8, feature_width), text_count, card_size, code_count)
-    gate_grad, up_grad, gain_sum, text_grad, code_sum = reduce_all(
-        normed, gate_back, up_back, gain_part, tables
+    weights, gain_sum, mine, last = reduce_all(normed, gate_back, up_back, gain_part, tables)
+    gate_grad, up_grad, text_grad, code_grad = results(
+        weights, mine, last, text_count // lax.axis_size("seq"), code_count
     )
     own_place = lax.axis_index("seq") * lax.axis_size("tp") + lax.axis_index("tp")
     gain_grad = lax.dynamic_slice_in_dim(gain_sum.reshape(-1), own_place * 8, 8)
-    code_grad = code_sum.reshape(code_count, -1, code_sum.shape[1])
     return (gate_grad, up_grad, gain_grad, text_grad, code_grad, context_grad)
 
 

time: 216 us -> 190 us (0.88)
  Pallas kernels: 203 us -> 185 us
  local copies, waits for them, and re-layouts: 9.22 us -> 2.6 us
    pallas_call x1 -> x2, Pallas kernels: 86.1 us -> 67.8 us  [the longest x1 65.5 us: reduce_all(): pl.pallas_call(reduce_kernel, out_shape=(jax.ShapeDtypeStruct((16, width)...]
    unnamed x8 -> x4, local copies, waits for them, and re-layouts: 7.95 us -> 1.33 us
where the time goes in v3:
time: 190 us
  Pallas kernels  185 us (97%)
  local copies, waits for them, and re-layouts  2.6 us (1%)
    pallas_call x1, Pallas kernels, front(): pl.pallas_call(front_kernel, out_shape=(jax.ShapeDtypeStruct((frames * 8,...  98.1 us
    pallas_call x1, Pallas kernels, reduce_all(): pl.pallas_call(reduce_kernel, out_shape=(jax.ShapeDtypeStruct((16, width)...  65.5 us
    pallas_call x1, Pallas kernels, scatter_rows(): pl.pallas_call(functools.partial(scatter_kernel, text_count=text_count, c...  18.8 us

profile of v3, /device:TPU:0, one launch (start us, length us, event | category | flops | bytes accessed | tf_op | source)
XLA Modules:
  0.0 189.6 jit_solution(13739275460485201575)
XLA Ops:
  0.6 0.8 add_bitcast_fusion.1
  1.5 0.7 add_bitcast_fusion
  2.2 0.6 copy.19
  2.8 98.1 %front.1 = (bf16[1024,1024]{1,0:T(8,128)(2,1)}, bf16[1024,2048]{1,0:T(8,128)(2,1)}, bf16[1024,2048]{1,0:T(8,128)(2,1)}, f32[8,128]{1,0:T(8,128)}, bf16[128,1024]...) custom-call(s32[8192]{0:T(1024)} %bitcast.15, bf16[16384,128]{1,0:T(8,128)(2,1)} %text_table.1, bf16[14336,128]{1,0:T(8,128)(2,1)} %bitcast.19, ...), custom_call_target="tpu_custom_call" | custom-call | flops 19000000512 | bytes 40000000 | tf_op jit(solution)/shard_map/front/pallas_call | solution.py:403
  100.9 18.8 %scatter_rows.1.tables = bf16[2,4,2,1920,128]{4,3,2,1,0:T(8,128)(2,1)} custom-call(s32[8192]{0:T(1024)} %bitcast.16, bf16[1024,8,128]{2,1,0:T(8,128)(2,1)} %bitcast.14), custom_call_target="tpu_custom_call" | custom-call | tf_op jit(solution)/shard_map/scatter_rows/pallas_call | solution.py:837
  119.8 0.0 copy-start
  119.8 65.5 %reduce_all.1 = (f32[16,2048]{1,0:T(8,128)}, f32[8,128]{1,0:T(8,128)}, bf16[1920,128]{1,0:T(8,128)(2,1)}, bf16[1920,128]{1,0:T(8,128)(2,1)}) custom-call(bf16[1024,1024]{1,0:T(8,128)(2,1)} %get-tuple-element.20.normed, bf16[1024,2048]{1,0:T(8,128)(2,1)} %get-tuple-element.21.gate_back, bf16[1024,2048]{1,0:T(8,128)(2,1)} %get-tuple-element.22.up_back, ...), custom_call_target="tpu_custom_call" | custom-call | flops 8999999488 | bytes 20000000 | tf_op jit(solution)/shard_map/reduce_all/pallas_call | solution.py:728
  185.3 2.3 %results.1 = (f32[8,2048]{1,0:T(8,128)}, f32[8,2048]{1,0:T(8,128)}, f32[1024,128]{1,0:T(8,128)}, f32[7,128,128]{2,1,0:T(8,128)}) custom-call(f32[16,2048]{1,0:T(8,128)} %get-tuple-element.25.weights, bf16[1920,128]{1,0:T(8,128)(2,1)} %get-tuple-element.26.mine, bf16[1920,128]{1,0:T(8,128)(2,1)} %get-tuple-element.27.last), custom_call_target="tpu_custom_call" | custom-call | tf_op jit(solution)/shard_map/results/pallas_call | solution.py:778
  187.6 1.3 dynamic_slice.3
  188.9 0.0 copy-done
  188.9 0.7 copy.21
  (1 shorter events, 0.0 us)
Async XLA Ops:
  119.8 69.1 %copy-start = (bf16[128,1024]{1,0:T(8,128)(2,1)S(1)}, bf16[128,1024]{1,0:T(8,128)(2,1)}, u32[]{:S(2)}) copy-start(bf16[128,1024]{1,0:T(8,128)(2,1)} %get-tuple-element.45) | copy-start | bytes 786436

commit v4 on v3

--- a/solution.py
+++ b/solution.py
@@ -37,10 +37,14 @@
 
 
 def greet(devices):
-    barrier = pltpu.get_barrier_semaphore()
     for device in devices:
-        pl.semaphore_signal(barrier, inc=1, device_id=device, device_id_type=MESH)
-    pl.semaphore_wait(barrier, len(devices))
+        pl.semaphore_signal(
+            pltpu.get_barrier_semaphore(), inc=1, device_id=device, device_id_type=MESH
+        )
+
+
+def greeted(devices):
+    pl.semaphore_wait(pltpu.get_barrier_semaphore(), len(devices))
 
 
 class Copies:
@@ -72,15 +76,20 @@
         self.pass_on, self.direct, self.ended = pass_on, direct, ended
 
     def first(self):
-        up, down, far = (step_to(self.here, by) for by in (1, 3, 2))
-        up_device, down_device = self.device(up), self.device(down)
+        for by in (2, 1, 3):
+            self.first_to(by)
+
+    def first_to(self, by):
+        there = step_to(self.here, by)
+        up_device, down_device = (self.device(step_to(self.here, to)) for to in (1, 3))
         send = self.copies.send
-        self.from_down = send(self.part(far, 0), self.pass_on(0), up_device)
-        self.from_up = send(self.part(far, 1), self.pass_on(1), down_device)
-        self.near = [
-            send(self.part(up, 1), self.direct(1), up_device),
-            send(self.part(down, 0), self.direct(0), down_device),
-        ]
+        if by == 2:
+            self.from_down = send(self.part(there, 0), self.pass_on(0), up_device)
+            self.from_up = send(self.part(there, 1), self.pass_on(1), down_device)
+        elif by == 1:
+            self.near = [send(self.part(there, 1), self.direct(1), up_device)]
+        else:
+            self.near.append(send(self.part(there, 0), self.direct(0), down_device))
 
     def second(self, add):
         up, down = step_to(self.here, 1), step_to(self.here, 3)
@@ -100,10 +109,9 @@
 
 
 class Exchange:
-    def __init__(self, copies, x, z_lo, device, chunk, landing, relay):
+    def __init__(self, copies, x, z_lo, device, chunk, landing):
         self.copies, self.x, self.z_lo, self.device = copies, x, z_lo, device
-        self.chunk, self.landing, self.relay = chunk, landing, relay
-        self.relays, self.arrivals = [], []
+        self.chunk, self.landing, self.arrivals = chunk, landing, []
 
     def place(self, by_x, by_z):
         z_lo = self.z_lo if by_z == 0 else 1 - self.z_lo
@@ -111,22 +119,9 @@
 
     def start(self, by_x, by_z):
         own, there = self.place(0, 0), self.place(by_x, by_z)
-        send = self.copies.send
-        if by_x == 2:
-            for half, by in ((0, 1), (1, 3)):
-                copy = send(self.chunk(there, half), self.relay(by_z, half), self.device(self.place(by, by_z)))
-                self.relays.append((copy, by_z, half))
-        else:
-            self.arrivals.append(send(self.chunk(there, None), self.landing(own, None), self.device(there)))
-
-    def forward(self):
-        for copy, by_z, half in self.relays:
-            copy.wait_recv()
-            came, by = ((3, 1), (1, 3))[half]
-            target = self.landing(self.place(came, by_z), half)
-            self.arrivals.append(
-                self.copies.send(self.relay(by_z, half), target, self.device(self.place(by, 0)))
-            )
+        self.arrivals.append(
+            self.copies.send(self.chunk(there), self.landing(own), self.device(there))
+        )
 
     def arrive(self):
         for copy in self.arrivals:
@@ -142,7 +137,7 @@
     normed_out, gate_out, up_out, gain_out, context_out, grid_out,
     table, staged, table_sems, picked,
     c_term, c_pass, c_direct, c_ended, c_pair, c_last, context,
-    e_send, e_in, e_relay, g_send, g_relay,
+    e_send, e_in, g_send,
     gate_w, up_w, hidden_in, stream_in, load_sems,
     normed, gate_back, up_back, out_sems, unit, scale, back, context_grad, gain_sum, send_sems, recv_sems,
 ):
@@ -153,7 +148,6 @@
     frames = frames_all // 8
     tile = frames // TILES
     rows = tile * 8
-    half_rows = rows // 2
     seq = lax.axis_index("seq")
     device = lambda place: (seq, place)
     copies = Copies(send_sems, recv_sems)
@@ -167,61 +161,89 @@
     block = staged.shape[1]
     text_blocks = text_table.shape[0] // block
     blocks = table.shape[0] // block
+    depth = staged.shape[0]
 
     def load_block(i):
         source = text_table if i < text_blocks else code_tables
         first = (i if i < text_blocks else i - text_blocks) * block
         return pltpu.make_async_copy(
-            source.at[pl.ds(first, block)], staged.at[i % 2], table_sems.at[i % 2]
+            source.at[pl.ds(first, block)], staged.at[i % depth], table_sems.at[i % depth]
         )
 
     block_loads = [load_block(i) for i in range(blocks)]
-    block_loads[0].start()
-    block_loads[1].start()
-    for load in loads:
-        load.start()
-    greet([device(lax.rem(own + by, 8)) for by in range(1, 8)])
-
-    def context_body(i, carry):
-        block_rows = pl.ds(pl.multiple_of(i * frames, frames), frames)
-        partial = jnp.dot(temporal[block_rows], context_weight[...], preferred_element_type=F32)
-        c_term[lax.div(i, 2), lax.rem(i, 2)] = partial.astype(BF16)
-        return carry
-
-    lax.fori_loop(0, 8, context_body, 0)
+    for i in range(depth):
+        block_loads[i].start()
+    others = [device(lax.rem(own + by, 8)) for by in range(1, 8)]
+    greet(others)
+
+    def context_part(at):
+        def body(low, carry):
+            block_rows = pl.ds(pl.multiple_of((at * 2 + low) * frames, frames), frames)
+            partial = jnp.dot(temporal[block_rows], context_weight[...], preferred_element_type=F32)
+            c_term[at, low] = partial.astype(BF16)
+            return carry
+
+        lax.fori_loop(0, 2, body, 0)
+
     half_width = c_term.shape[-1] // 2
+    half_frames = frames // 2
     c_half = lambda half: pl.ds(half * half_width, half_width)
-    c_pick = lambda ref: lambda half: ref.at[:, :, c_half(half)]
-    c_ring = Ring(
-        copies, x, lambda at: device(at * 2 + z_lo),
-        lambda at, half: c_term.at[at, :, :, c_half(half)],
-        c_pick(c_pass), c_pick(c_direct), c_pick(c_ended),
-    )
-    c_ring.first()
+    c_frames = [pl.ds(h * half_frames, half_frames) for h in range(2)]
+
+    def context_ring(h):
+        pick = lambda ref: lambda half: ref.at[:, c_frames[h], c_half(half)]
+        return Ring(
+            copies, x, lambda at: device(at * 2 + z_lo),
+            lambda at, half: c_term.at[at, :, c_frames[h], c_half(half)],
+            pick(c_pass), pick(c_direct), pick(c_ended),
+        )
+
+    c_rings = [context_ring(h) for h in range(2)]
 
     def add_context(out, refs):
         def body(i, carry):
-            at = pl.ds(pl.multiple_of(lax.rem(i, frames // 16) * 16, 16), 16)
-            low = lax.div(i, frames // 16)
-            total = refs[0][low, at].astype(F32)
-            for ref in refs[1:]:
-                total = total + ref[low, at].astype(F32)
-            out[low, at] = total.astype(BF16)
-            return carry
-
-        lax.fori_loop(0, frames // 8, body, 0)
+            at = pl.ds(pl.multiple_of(lax.rem(i, half_frames // 16) * 16, 16), 16)
+            low = lax.div(i, half_frames // 16)
+            out[low, at] = total_of([ref.at[low, at] for ref in refs]).astype(BF16)
+            return carry
+
+        lax.fori_loop(0, frames // 16, body, 0)
+
+    def context_pair(h):
+        c_rings[h].third(add_context, lambda half: c_pair.at[:, c_frames[h], c_half(half)])
+        there = device(x * 2 + 1 - z_lo)
+        return copies.send(c_pair.at[1 - z_lo, c_frames[h]], c_last.at[c_frames[h]], there)
+
+    def context_total(h, copy):
+        copy.wait_recv()
+
+        def body(i, carry):
+            at = pl.ds(pl.multiple_of(h * half_frames + i * 16, 16), 16)
+            context[at] = total_of([c_pair.at[z_lo, at], c_last.at[at]])
+            return carry
+
+        lax.fori_loop(0, half_frames // 16, body, 0)
+
+    context_part(step_to(x, 2))
+    greeted(others)
+    for by in (2, 1, 3):
+        c_rings[0].first_to(by)
+        context_part(step_to(x, {2: 1, 1: 3, 3: 0}[by]))
 
     for i in range(blocks):
         block_loads[i].wait()
 
         def widen(j, carry):
             at = pl.multiple_of(j * 128, 128)
-            table[pl.ds(i * block + at, 128)] = staged[i % 2, pl.ds(at, 128)].astype(F32)
+            table[pl.ds(i * block + at, 128)] = staged[i % depth, pl.ds(at, 128)].astype(F32)
             return carry
 
         lax.fori_loop(0, block // 128, widen, 0)
-        if i + 2 < blocks:
-            block_loads[i + 2].start()
+        if i + depth < blocks:
+            block_loads[i + depth].start()
+        if i == blocks - depth:
+            for load in loads:
+                load.start()
 
     def gather(t, place, target):
         def body(f, carry):
@@ -233,49 +255,43 @@
         lax.fori_loop(0, tile, body, 0, unroll=4)
         target[...] = picked[...].astype(BF16)
 
-    def tile_rows(t, half):
-        if half is None:
-            return pl.ds(t * rows, rows)
-        return pl.ds(t * rows + half * half_rows, half_rows)
-
-    def exchange(t, send_ref, in_ref, relay_ref):
+    def tile_rows(t):
+        return pl.ds(t * rows, rows)
+
+    def exchange(t, send_ref, in_ref):
         return Exchange(
             copies, x, z_lo, device,
-            lambda place, half: send_ref.at[place, tile_rows(t, half)],
-            lambda place, half: in_ref.at[place, tile_rows(t, half)],
-            lambda by_z, half: relay_ref.at[t, by_z, half],
+            lambda place: send_ref.at[place, tile_rows(t)],
+            lambda place: in_ref.at[place, tile_rows(t)],
         )
 
-    rows_in = [exchange(t, e_send, e_in, e_relay) for t in range(TILES)]
-    rows_back = [exchange(t, g_send, grid_out, g_relay) for t in range(TILES)]
+    rows_in = [exchange(t, e_send, e_in) for t in range(TILES)]
+    rows_back = [exchange(t, g_send, grid_out) for t in range(TILES)]
 
     def gather_tile(t):
         for by_x, by_z in ORDER:
             place = rows_in[t].place(by_x, by_z)
             if (by_x, by_z) == (0, 0):
-                gather(t, place, e_in.at[place, tile_rows(t, None)])
+                gather(t, place, e_in.at[place, tile_rows(t)])
             else:
-                gather(t, place, e_send.at[place, tile_rows(t, None)])
-                rows_in[t].start(by_x, by_z)
+                gather(t, place, e_send.at[place, tile_rows(t)])
+
+    def send_tile(t):
+        for by_x, by_z in ORDER[:-1]:
+            rows_in[t].start(by_x, by_z)
 
     gather_tile(0)
-    c_ring.second(add_context)
+    c_rings[0].second(add_context)
+    send_tile(0)
+    c_rings[1].first()
     gather_tile(1)
-    rows_in[0].forward()
-    c_ring.third(add_context, lambda half: c_pair.at[:, :, c_half(half)])
-    c_copy = copies.send(c_pair.at[1 - z_lo], c_last, device(x * 2 + 1 - z_lo))
+    c_copy = context_pair(0)
+    send_tile(1)
     gather_tile(2)
-    rows_in[1].forward()
+    c_rings[1].second(add_context)
+    send_tile(2)
     gather_tile(3)
-    rows_in[2].forward()
-    c_copy.wait_recv()
-
-    def context_total(i, carry):
-        at = pl.ds(pl.multiple_of(i * 16, 16), 16)
-        context[at] = c_pair[z_lo, at].astype(F32) + c_last[at].astype(F32)
-        return carry
-
-    lax.fori_loop(0, frames // 16, context_total, 0)
+    context_total(0, c_copy)
 
     width = context.shape[1]
     column_blocks = width // 128
@@ -366,22 +382,20 @@
         return outs
 
     outs = [run_tile(0)]
-    rows_in[3].forward()
+    c_copy = context_pair(1)
+    send_tile(3)
     outs.append(run_tile(1))
-    rows_back[0].forward()
     for out in outs[0]:
         out.wait()
+    context_total(1, c_copy)
     outs.append(run_tile(2))
-    rows_back[1].forward()
     for out in outs[1]:
         out.wait()
     outs.append(run_tile(3))
-    rows_back[2].forward()
     context_out[...] = context_grad[...].astype(BF16)
     gain_row = jnp.sum(gain_sum[...], axis=0, keepdims=True)
     for j in range(8):
         gain_out[j : j + 1] = gain_row[:, j * 128 : (j + 1) * 128]
-    rows_back[3].forward()
     for out in outs[2] + outs[3]:
         out.wait()
     for t in range(TILES):
@@ -414,16 +428,15 @@
         + [anywhere] * 4,
         out_specs=(anywhere, anywhere, anywhere, vmem, vmem, vmem),
         scratch_shapes=[
-            f32(table_rows, 128), bf(2, 2048, 128), dma(2), f32(rows, 128),
+            f32(table_rows, 128), bf(6, 2048, 128), dma(6), f32(rows, 128),
             bf(4, 2, frames, width), bf(2, frames, width), bf(2, frames, width), bf(2, frames, width),
             bf(2, frames, width), bf(frames, width), f32(frames, width),
-            bf(8, frames * 8, 128), bf(8, frames * 8, 128), bf(TILES, 2, 2, rows // 2, 128),
-            bf(8, frames * 8, 128), bf(TILES, 2, 2, rows // 2, 128),
+            bf(8, frames * 8, 128), bf(8, frames * 8, 128), bf(8, frames * 8, 128),
             bf(width, hidden_width), bf(width, hidden_width),
             bf(frames * 8, hidden_width), bf(frames * 8, width), dma(4),
             bf(2, rows, width), bf(2, rows, hidden_width), bf(2, rows, hidden_width), dma(2, 3),
             f32(rows, width), f32(rows, 128), f32(rows, width), f32(frames, width), f32(8, width),
-            dma(120), dma(120),
+            dma(128), dma(128),
         ],
         compiler_params=pltpu.CompilerParams(
             collective_id=2, has_side_effects=True, vmem_limit_bytes=VMEM_LIMIT
@@ -480,23 +493,25 @@
     ]
     for load in loads + keeps:
         load.start()
-    greet(
+    partners = (
         [sibling]
         + [x_device(step_to(x, by)) for by in (1, 2, 3)]
         + [y_device(step_to(y, by)) for by in (1, 2, 3)]
         + [z_device(step_to(z, by)) for by in (1, 2, 3)]
     )
+    greet(partners)
+    greeted(partners)
     copies = Copies(send_sems, recv_sems)
 
-    table_pairs = [
-        [
+    def send_tables(c):
+        return [
             copies.send(tables.at[1 - core, i, :, t_rows(c)], other.at[i, :, t_rows(c)], sibling)
             for i in range(4)
         ]
-        for c in range(CHUNKS)
-    ]
+
     gain_own[0] = gain[...]
     gain_copy = copies.send(gain_own.at[0], gain_in.at[0], sibling)
+    table_pairs = [send_tables(c) for c in range(CHUNKS)]
 
     def make_term(q):
         turned[:128] = left_in[:, q * 128 : (q + 1) * 128].T
@@ -643,36 +658,38 @@
             total = total + gain_in[slot]
         return total
 
+    pair_tables(0)
     for load in loads:
         load.wait()
     make_term(0)
     send_pair(0)
-    pair_tables(0)
+    gain_sum = gain_total([gain_copy], [0])
+    gain_copies = gain_round(1, x_device, x)
     pair_tables(1)
+    pair_tables(2)
     make_term(1)
     send_pair(1)
-    pair_tables(2)
+    gain_sum = gain_total(gain_copies, [1, 2, 3])
+    gain_copies = gain_round(2, z_device, z)
     first_start(0)
     t_rings[0].second(add_tables)
-    gain_sum = gain_total([gain_copy], [0])
-    gain_copies = gain_round(1, x_device, x)
     make_term(2)
     send_pair(2)
+    gain_sum = gain_total(gain_copies, [4, 5, 6])
+    gain_copies = gain_round(3, y_device, y)
     first_start(1)
     first_middle(0)
-    t_rings[1].second(add_tables)
     make_term(3)
     send_pair(3)
+    t_rings[1].second(add_tables)
     first_start(2)
     first_middle(1)
     first_out(0)
-    gain_sum = gain_total(gain_copies, [1, 2, 3])
-    gain_copies = gain_round(2, y_device, y)
+    t_rings[2].second(add_tables)
     first_start(3)
     first_middle(2)
     first_out(1)
     second_middle(0)
-    t_rings[2].second(add_tables)
     tables_out(0)
     first_middle(3)
     first_out(2)
@@ -680,13 +697,11 @@
     second_out(0)
     tables_out(1)
     tables_relay(0)
-    gain_sum = gain_total(gain_copies, [4, 5, 6])
-    gain_copies = gain_round(3, z_device, z)
     first_out(3)
     second_middle(2)
     second_out(1)
+    tables_out(2)
     tables_relay(1)
-    tables_out(2)
     second_middle(3)
     second_out(2)
     second_out(3)

time: 190 us -> 176 us (0.926)
  Pallas kernels: 185 us -> 171 us
    pallas_call x1, Pallas kernels: 98.1 us -> 85.8 us  [front(): pl.pallas_call(front_kernel, out_shape=(jax.ShapeDtypeStruct((frames * 8,...]
where the time goes in v4:
time: 176 us
  Pallas kernels  171 us (97%)
  local copies, waits for them, and re-layouts  2.6 us (1%)
    pallas_call x1, Pallas kernels, front(): pl.pallas_call(front_kernel, out_shape=(jax.ShapeDtypeStruct((frames * 8,...  85.8 us
    pallas_call x1, Pallas kernels, reduce_all(): pl.pallas_call(reduce_kernel, out_shape=(jax.ShapeDtypeStruct((16, width)...  63.8 us
    pallas_call x1, Pallas kernels, scatter_rows(): pl.pallas_call(functools.partial(scatter_kernel, text_count=text_count, c...  18.8 us

profile of v4, /device:TPU:0, one launch (start us, length us, event | category | flops | bytes accessed | tf_op | source)
XLA Modules:
  0.0 175.6 jit_solution(9341480102945908504)
XLA Ops:
  0.6 0.8 add_bitcast_fusion.1
  1.5 0.7 add_bitcast_fusion
  2.2 0.6 copy.19
  2.8 85.8 %front.1 = (bf16[1024,1024]{1,0:T(8,128)(2,1)}, bf16[1024,2048]{1,0:T(8,128)(2,1)}, bf16[1024,2048]{1,0:T(8,128)(2,1)}, f32[8,128]{1,0:T(8,128)}, bf16[128,1024]...) custom-call(s32[8192]{0:T(1024)} %bitcast.15, bf16[16384,128]{1,0:T(8,128)(2,1)} %text_table.1, bf16[14336,128]{1,0:T(8,128)(2,1)} %bitcast.19, ...), custom_call_target="tpu_custom_call" | custom-call | flops 19000000512 | bytes 40000000 | tf_op jit(solution)/shard_map/front/pallas_call | solution.py:417
  88.6 18.8 %scatter_rows.1.tables = bf16[2,4,2,1920,128]{4,3,2,1,0:T(8,128)(2,1)} custom-call(s32[8192]{0:T(1024)} %bitcast.16, bf16[1024,8,128]{2,1,0:T(8,128)(2,1)} %bitcast.14), custom_call_target="tpu_custom_call" | custom-call | tf_op jit(solution)/shard_map/scatter_rows/pallas_call | solution.py:852
  107.5 0.0 copy-start
  107.5 63.8 %reduce_all.1 = (f32[16,2048]{1,0:T(8,128)}, f32[8,128]{1,0:T(8,128)}, bf16[1920,128]{1,0:T(8,128)(2,1)}, bf16[1920,128]{1,0:T(8,128)(2,1)}) custom-call(bf16[1024,1024]{1,0:T(8,128)(2,1)} %get-tuple-element.20.normed, bf16[1024,2048]{1,0:T(8,128)(2,1)} %get-tuple-element.21.gate_back, bf16[1024,2048]{1,0:T(8,128)(2,1)} %get-tuple-element.22.up_back, ...), custom_call_target="tpu_custom_call" | custom-call | flops 8999999488 | bytes 20000000 | tf_op jit(solution)/shard_map/reduce_all/pallas_call | solution.py:743
  171.3 2.3 %results.1 = (f32[8,2048]{1,0:T(8,128)}, f32[8,2048]{1,0:T(8,128)}, f32[1024,128]{1,0:T(8,128)}, f32[7,128,128]{2,1,0:T(8,128)}) custom-call(f32[16,2048]{1,0:T(8,128)} %get-tuple-element.25.weights, bf16[1920,128]{1,0:T(8,128)(2,1)} %get-tuple-element.26.mine, bf16[1920,128]{1,0:T(8,128)(2,1)} %get-tuple-element.27.last), custom_call_target="tpu_custom_call" | custom-call | tf_op jit(solution)/shard_map/results/pallas_call | solution.py:793
  173.6 1.3 dynamic_slice.3
  174.9 0.0 copy-done
  174.9 0.7 copy.21
  (1 shorter events, 0.0 us)
Async XLA Ops:
  107.5 67.4 %copy-start = (bf16[128,1024]{1,0:T(8,128)(2,1)S(1)}, bf16[128,1024]{1,0:T(8,128)(2,1)}, u32[]{:S(2)}) copy-start(bf16[128,1024]{1,0:T(8,128)(2,1)} %get-tuple-element.45) | copy-start | bytes 786436

commit v5 on v4

--- a/solution.py
+++ b/solution.py
@@ -252,7 +252,7 @@
                 picked[pl.ds(f * 8 + k, 1)] = table[pl.ds(ids[k * frames_all + frame], 1)]
             return carry
 
-        lax.fori_loop(0, tile, body, 0, unroll=4)
+        lax.fori_loop(0, tile, body, 0, unroll=16)
         target[...] = picked[...].astype(BF16)
 
     def tile_rows(t):
@@ -659,13 +659,13 @@
         return total
 
     pair_tables(0)
+    pair_tables(1)
     for load in loads:
         load.wait()
     make_term(0)
     send_pair(0)
     gain_sum = gain_total([gain_copy], [0])
     gain_copies = gain_round(1, x_device, x)
-    pair_tables(1)
     pair_tables(2)
     make_term(1)
     send_pair(1)
@@ -679,9 +679,9 @@
     gain_copies = gain_round(3, y_device, y)
     first_start(1)
     first_middle(0)
+    t_rings[1].second(add_tables)
     make_term(3)
     send_pair(3)
-    t_rings[1].second(add_tables)
     first_start(2)
     first_middle(1)
     first_out(0)
@@ -832,7 +832,7 @@
             total[pl.ds(places[k], 1)] = sums[k]
         return carry
 
-    lax.fori_loop(0, frames, body, 0, unroll=4)
+    lax.fori_loop(0, frames, body, 0, unroll=16)
 
     text_block, code_block = text_count // 16, card // 16
     for block in range(16):

time: 176 us -> 175 us (level)
  no operation moved by 1% of the time
where the time goes in v5:
time: 175 us
  Pallas kernels  170 us (97%)
  local copies, waits for them, and re-layouts  2.6 us (1%)
    pallas_call x1, Pallas kernels, front(): pl.pallas_call(front_kernel, out_shape=(jax.ShapeDtypeStruct((frames * 8,...  85.4 us
    pallas_call x1, Pallas kernels, reduce_all(): pl.pallas_call(reduce_kernel, out_shape=(jax.ShapeDtypeStruct((16, width)...  64 us
    pallas_call x1, Pallas kernels, scatter_rows(): pl.pallas_call(functools.partial(scatter_kernel, text_count=text_count, c...  18.6 us

profile of v5, /device:TPU:0, one launch (start us, length us, event | category | flops | bytes accessed | tf_op | source)
XLA Modules:
  0.0 175.0 jit_solution(4791968924189952653)
XLA Ops:
  0.6 0.8 add_bitcast_fusion.1
  1.5 0.7 add_bitcast_fusion
  2.2 0.6 copy.19
  2.8 85.4 %front.1 = (bf16[1024,1024]{1,0:T(8,128)(2,1)}, bf16[1024,2048]{1,0:T(8,128)(2,1)}, bf16[1024,2048]{1,0:T(8,128)(2,1)}, f32[8,128]{1,0:T(8,128)}, bf16[128,1024]...) custom-call(s32[8192]{0:T(1024)} %bitcast.15, bf16[16384,128]{1,0:T(8,128)(2,1)} %text_table.1, bf16[14336,128]{1,0:T(8,128)(2,1)} %bitcast.19, ...), custom_call_target="tpu_custom_call" | custom-call | flops 19000000512 | bytes 40000000 | tf_op jit(solution)/shard_map/front/pallas_call | solution.py:417
  88.2 18.6 %scatter_rows.1.tables = bf16[2,4,2,1920,128]{4,3,2,1,0:T(8,128)(2,1)} custom-call(s32[8192]{0:T(1024)} %bitcast.16, bf16[1024,8,128]{2,1,0:T(8,128)(2,1)} %bitcast.14), custom_call_target="tpu_custom_call" | custom-call | tf_op jit(solution)/shard_map/scatter_rows/pallas_call | solution.py:852
  106.7 0.0 copy-start
  106.7 64.0 %reduce_all.1 = (f32[16,2048]{1,0:T(8,128)}, f32[8,128]{1,0:T(8,128)}, bf16[1920,128]{1,0:T(8,128)(2,1)}, bf16[1920,128]{1,0:T(8,128)(2,1)}) custom-call(bf16[1024,1024]{1,0:T(8,128)(2,1)} %get-tuple-element.20.normed, bf16[1024,2048]{1,0:T(8,128)(2,1)} %get-tuple-element.21.gate_back, bf16[1024,2048]{1,0:T(8,128)(2,1)} %get-tuple-element.22.up_back, ...), custom_call_target="tpu_custom_call" | custom-call | flops 8999999488 | bytes 20000000 | tf_op jit(solution)/shard_map/reduce_all/pallas_call | solution.py:743
  170.7 2.3 %results.1 = (f32[8,2048]{1,0:T(8,128)}, f32[8,2048]{1,0:T(8,128)}, f32[1024,128]{1,0:T(8,128)}, f32[7,128,128]{2,1,0:T(8,128)}) custom-call(f32[16,2048]{1,0:T(8,128)} %get-tuple-element.25.weights, bf16[1920,128]{1,0:T(8,128)(2,1)} %get-tuple-element.26.mine, bf16[1920,128]{1,0:T(8,128)(2,1)} %get-tuple-element.27.last), custom_call_target="tpu_custom_call" | custom-call | tf_op jit(solution)/shard_map/results/pallas_call | solution.py:793
  173.0 1.3 dynamic_slice.3
  174.3 0.0 copy-done
  174.3 0.7 copy.21
  (1 shorter events, 0.0 us)
Async XLA Ops:
  106.7 67.6 %copy-start = (bf16[128,1024]{1,0:T(8,128)(2,1)S(1)}, bf16[128,1024]{1,0:T(8,128)(2,1)}, u32[]{:S(2)}) copy-start(bf16[128,1024]{1,0:T(8,128)(2,1)} %get-tuple-element.45) | copy-start | bytes 786436
